TPU v7x, 32 devices: a whole 2x2x4 slice. The times are simulated.
32 devices in a mesh: groups: 2 (over y), wide: 4 (over z), narrow: 4 (over x, core).
Axes of the slice: x: 2, y: 2, z: 4, core: 2. Of those that a mesh axis runs over, the one named last changes fastest.
Arguments:
- inputs: bfloat16 [40, 2, 8192], P('groups', None, 'narrow'), parts along dimension 0, may hold values from -6 to 6
- xz_weight: bfloat16 [8192, 2, 16384], P('narrow', None, 'wide'), may hold values from -0.0625 to 0.0625
- bc_weight: bfloat16 [8192, 4096], P('narrow', 'wide'), may hold values from -0.0625 to 0.0625
- dt_weight: bfloat16 [8192, 256], P('narrow', 'wide'), may hold values from -0.0625 to 0.0625
- conv_x_weight: bfloat16 [4, 256, 64], P(None, 'wide', 'narrow'), may hold values from -3 to 3
- conv_x_bias: bfloat16 [256, 64], P('wide', 'narrow'), may hold values from -3 to 3
- conv_bc_weight: bfloat16 [4, 4096], P(None, 'wide'), may hold values from -3 to 3
- conv_bc_bias: bfloat16 [4096], P('wide'), may hold values from -3 to 3
- conv_x_state: bfloat16 [40, 3, 256, 64], P('groups', None, 'wide', 'narrow'), parts along dimension 0, may hold values from -6 to 6
- conv_bc_state: bfloat16 [40, 3, 4096], P('groups', None, 'wide'), parts along dimension 0, may hold values from -6 to 6
- dt_bias: float32 [256], P('wide'), may hold values from -4 to 0
- a_log: float32 [256], P('wide'), may hold values from 0 to 2.5
- d_skip: float32 [256], P('wide'), may hold values from 0.5 to 2
- norm_weight: bfloat16 [256, 64], P('wide', 'narrow'), may hold values from 0.099609375 to 1.8984375
- out_weight: bfloat16 [256, 64, 8192], P(None, 'narrow', 'wide'), may hold values from -0.046875 to 0.046875
- ssm_state: float32 [40, 256, 64, 256], P('groups', 'wide', 'narrow'), parts along dimension 0, may hold values from -4 to 4
Outputs:
- layer_out: bfloat16 [40, 2, 8192], P('groups', None, ('wide', 'narrow')), parts along dimension 0
- new_ssm_state: float32 [40, 256, 64, 256], P('groups', 'wide', 'narrow'), parts along dimension 0
- new_conv_x: bfloat16 [40, 3, 256, 64], P('groups', None, 'wide', 'narrow'), parts along dimension 0
- new_conv_bc: bfloat16 [40, 3, 4096], P('groups', None, 'wide'), parts along dimension 0
There are 2 independent parts, one for each index of `groups`. A program takes and returns all parts, laid end to end along the dimension named above; an argument that names none is the same for every part. Nothing has to cross between parts.
All inputs are finite; a program needn't handle non-finite values.
Results may differ from a plain program's by a relative error of at most 0.015.
Values may be sent and summed in bfloat16 or wider, within the bound.
No kernel may reach another device: no remote copies, remote signals or barrier semaphores. Data moves between devices by JAX's collectives and lax.ppermute only.
A program may use at most 192 MiB of HBM per device.

v0:
```python
import jax
import jax.numpy as jnp
from jax import lax
from jax.sharding import PartitionSpec as P

HEADS = 256
HEAD_DIM = 64
STATE = 256
NGROUPS = 8


EPSILON = 1e-05


def shortened(value):

    def short(part):
        return part.astype(jnp.bfloat16) if part.dtype == jnp.float32 else part

    return jax.tree.map(short, value)


def swapped(value, axis, bit):
    mask = 2**bit
    pairs = [(source, source ^ mask) for source in range(lax.axis_size(axis))]
    return lax.ppermute(value, axis, pairs)


def conv_tokens(history, fresh_vals, tap_weights, offset):
    window = jnp.concatenate([history, fresh_vals], axis=1)
    outputs = []
    for token_idx in range(2):
        summed = offset.astype(jnp.float32)
        for tap_idx in range(tap_weights.shape[0]):
            summed = summed + tap_weights[tap_idx].astype(jnp.float32) * window[
                :, token_idx + tap_idx
            ].astype(jnp.float32)
        outputs.append(jax.nn.silu(summed))
    return (jnp.stack(outputs, axis=1), window[:, 2:])


def advance(ssm_now, x_tok, b_tok, c_tok, dt_tok, dt_bias, a_log, d_skip):
    step_size = jax.nn.softplus(dt_tok.astype(jnp.float32) + dt_bias)
    decay_now = jnp.exp(-step_size * jnp.exp(a_log))
    inject = (step_size[:, :, None] * x_tok)[..., None] * b_tok[:, :, None, :]
    ssm_now = decay_now[:, :, None, None] * ssm_now + inject
    readout = jnp.sum(ssm_now * c_tok[:, :, None, :], axis=-1) + d_skip[None, :, None] * x_tok
    return (ssm_now, readout)


def shards(
    inputs,
    xz_weight,
    bc_weight,
    dt_weight,
    conv_x_weight,
    conv_x_bias,
    conv_bc_weight,
    conv_bc_bias,
    conv_x_state,
    conv_bc_state,
    dt_bias,
    a_log,
    d_skip,
    norm_weight,
    out_weight,
    ssm_state,
):
    seq_count = inputs.shape[0]
    row_count = seq_count * 2
    tok_rows = inputs.reshape(row_count, inputs.shape[2])
    head_local = dt_weight.shape[1]
    wide_count = lax.axis_size("wide")
    narrow_count = lax.axis_size("narrow")
    wide_index = lax.axis_index("wide")
    chan_local = HEAD_DIM // narrow_count
    xz_local = xz_weight.reshape(xz_weight.shape[0], 2, head_local, HEAD_DIM)
    bc_part = jnp.dot(tok_rows, bc_weight, preferred_element_type=jnp.float32)
    dt_part = jnp.dot(tok_rows, dt_weight, preferred_element_type=jnp.float32)
    xz_mine = lax.psum_scatter(
        jnp.einsum("rd,dzhc->czrh", tok_rows, xz_local, preferred_element_type=jnp.float32),
        "narrow",
        scatter_dimension=0,
        tiled=True,
    )
    bc_summed, dt_summed = lax.psum((bc_part, dt_part), "narrow")
    xz_mine = xz_mine.astype(jnp.bfloat16)
    xz_mine = jnp.transpose(xz_mine, (1, 2, 3, 0)).reshape(2, seq_count, 2, head_local, chan_local)
    gate_vals = xz_mine[0]
    x_proj = xz_mine[1]
    bc_proj = bc_summed.astype(jnp.bfloat16).reshape(seq_count, 2, bc_summed.shape[1])
    dt_proj = dt_summed.astype(jnp.bfloat16).reshape(seq_count, 2, head_local)
    x_conv, new_conv_x = conv_tokens(conv_x_state, x_proj, conv_x_weight, conv_x_bias)
    bc_conv, new_conv_bc = conv_tokens(conv_bc_state, bc_proj, conv_bc_weight, conv_bc_bias)
    group_local = max(NGROUPS // wide_count, 1)
    group_span = max(wide_count // NGROUPS, 1)
    bc_mine = bc_conv.reshape(row_count, bc_conv.shape[2])
    for bit_idx in range(group_span.bit_length() - 1):
        partner = swapped(shortened(bc_mine), "wide", bit_idx).astype(bc_mine.dtype)
        is_lower = wide_index // (1 << bit_idx) % 2 == 0
        bc_mine = jnp.where(
            is_lower,
            jnp.concatenate([bc_mine, partner], axis=1),
            jnp.concatenate([partner, bc_mine], axis=1),
        )
    bc_heads = bc_mine.reshape(seq_count, 2, group_local, 2, STATE)
    per_group = head_local // group_local
    b_heads = jnp.repeat(bc_heads[:, :, :, 0], per_group, axis=2)
    c_heads = jnp.repeat(bc_heads[:, :, :, 1], per_group, axis=2)
    ssm_now = ssm_state
    readouts = []
    for token_idx in range(2):
        ssm_now, readout = advance(
            ssm_now,
            x_conv[:, token_idx],
            b_heads[:, token_idx],
            c_heads[:, token_idx],
            dt_proj[:, token_idx],
            dt_bias,
            a_log,
            d_skip,
        )
        readouts.append(readout)
    y_all = jnp.stack(readouts, axis=1)
    gated_out = y_all * jax.nn.silu(gate_vals.astype(jnp.float32))
    grouped = gated_out.reshape(seq_count, 2, group_local, per_group * chan_local)
    squares_part = jnp.sum(grouped * grouped, axis=-1)
    group_sum = lax.psum(squares_part, "narrow")
    for bit_idx in range(group_span.bit_length() - 1):
        group_sum = group_sum + swapped(group_sum, "wide", bit_idx)
    inverse = lax.rsqrt(group_sum / (HEADS // NGROUPS * HEAD_DIM) + EPSILON)
    normed = (grouped * inverse[..., None]).reshape(
        seq_count, 2, head_local, chan_local
    ) * norm_weight.astype(jnp.float32)
    normed = normed.astype(jnp.bfloat16).reshape(row_count, head_local, chan_local)
    out_part = jnp.einsum(
        "rhc,hcd->rd",
        lax.all_gather(normed, "wide", axis=1, tiled=True),
        out_weight,
        preferred_element_type=jnp.float32,
    )
    out_mine = lax.psum_scatter(
        out_part.astype(jnp.bfloat16), "narrow", scatter_dimension=1, tiled=True
    )
    layer_out = out_mine.reshape(seq_count, 2, out_mine.shape[1])
    return (layer_out, ssm_now, new_conv_x, new_conv_bc)


def solution(mesh):
    return jax.shard_map(
        shards,
        mesh=mesh,
        in_specs=(
            P("groups", None, "narrow"),
            P("narrow", None, "wide"),
            P("narrow", "wide"),
            P("narrow", "wide"),
            P(None, "wide", "narrow"),
            P("wide", "narrow"),
            P(None, "wide"),
            P("wide"),
            P("groups", None, "wide", "narrow"),
            P("groups", None, "wide"),
            P("wide"),
            P("wide"),
            P("wide"),
            P("wide", "narrow"),
            P(None, "narrow", "wide"),
            P("groups", "wide", "narrow", None),
        ),
        out_specs=(
            P("groups", None, ("wide", "narrow")),
            P("groups", "wide", "narrow", None),
            P("groups", None, "wide", "narrow"),
            P("groups", None, "wide"),
        ),
        check_vma=False,
    )
```

profile of v0, /device:TPU:0, one launch (start us, length us, event | category | flops | bytes accessed | tf_op | source)
XLA Modules:
  0.0 251.0 jit_solution(5239584444995894743)
XLA Ops:
  7.2 80.9 %copy.186 = bf16[2048,2,4096]{0,2,1:T(8,128)(2,1)} copy(bf16[2048,2,4096]{2,1,0:T(2,128)(2,1)} %param.17) | data formatting | bytes 67108864 | tf_op args[1]
  88.3 21.7 %convolution_bitcast_fusion.1 = f32[64,2,40,64]{0,2,3,1:T(8,128)S(1)} fusion(bf16[2048,2,64,64]{0,3,2,1:T(8,128)(2,1)} %bitcast.177, bf16[40,2048,1,1]{1,0,2,3:T(8,128)(2,1)S(1)} %reshape.347), kind=kOutput, calls=%fused_computation.6 | convolution fusion | flops 1342177280 | bytes 35028992 | tf_op jit(solution)/shard_map/rd,dzhc->czrh/dot_general | solution.py:81
  110.0 2.1 copy.187
  112.2 3.0 %fusion.60 = f32[40,1024]{1,0:T(8,128)S(1)} fusion(bf16[40,2048]{1,0:T(8,128)(2,1)S(1)} %reshape.324, bf16[2048,1024]{1,0:T(8,128)(2,1)} %param.18), kind=kOutput, calls=%fused_computation.124 | convolution fusion | flops 167772160 | bytes 4521984 | tf_op jit(solution)/shard_map/dot_general | solution.py:78
  115.5 15.5 %all-reduce.2 = (bf16[40,1024]{1,0:T(8,128)(2,1)S(1)}, bf16[40,64]{1,0:T(8,128)(2,1)S(1)}) all-reduce(f32[40,1024]{1,0:T(8,128)S(1)} %fusion.60, f32[40,64]{1,0:T(8,128)S(1)} %fusion.59), channel_id=1, replica_groups=mesh['groups'=2,'wide'=4,'narrow'=4] {'narrow'}, use_global_device_ids=true, to_apply=%region_2.0 | all-reduce | flops 43520 | bytes 261120 | tf_op jit(solution)/shard_map/psum | solution.py:86
  131.6 1.0 divide_multiply_fusion
  133.3 0.9 copy.214
  134.2 0.7 copy.185
  134.9 0.7 copy.183
  135.6 0.7 copy.181
  136.2 0.7 copy.179
  136.9 1.4 copy.178
  139.0 1.3 convert_element_type.253
  140.3 1.3 multiply_exponential_fusion
  142.5 1.8 slice_bitcast_fusion.3
  144.3 5.2 %reduce-scatter.3.cloned.1.call-done = f32[16,2,40,64]{3,2,1,0:T(8,128)} async-done(((f32[64,2,40,64]{3,2,1,0:T(8,128)}), f32[16,2,40,64]{3,2,1,0:T(8,128)}) %reduce-scatter.3.cloned.1.call-update) | async-done | bytes 327696 | tf_op jit(solution)/shard_map/reduce_scatter | solution.py:80
  149.6 1.3 copy.234
  150.9 0.7 copy-done.4
  153.0 1.8 copy.217
  154.8 1.8 copy.218
  156.5 2.0 multiply_multiply_fusion.1
  158.6 21.2 %multiply_reduce_fusion = (f32[20,64,16]{2,1,0:T(8,128)S(1)}, f32[20,64,16,256]{3,2,1,0:T(8,128)}, f32[20,64,16]{2,1,0:T(8,128)S(1)}) fusion(f32[20,64,256]{2,1,0:T(8,128)S(1)} %get-tuple-element.10, f32[20,64,256]{2,1,0:T(8,128)} %get-tuple-element.12, f32[20,64,16]{2,1,0:T(8,128)S(1)} %get-tuple-element.16, f32[20,64,256]{2,1,0:T(8,128)} %get-tuple-element.11, ...), kind=kLoop, calls=%fused_computation | loop fusion | flops 52387840 | bytes 47523840 | tf_op jit(solution)/shard_map/reduce_sum | solution.py:47
  179.9 0.8 bitcast_add_fusion.1
  182.8 1.1 fusion.40
  184.3 5.7 %psum.23 = f32[20,2,2]{0,2,1:T(2,128)S(1)} all-reduce(f32[20,2,2]{0,2,1:T(2,128)S(1)} %copy.204), channel_id=1, replica_groups=mesh['groups'=2,'wide'=4,'narrow'=4] {'narrow'}, use_global_device_ids=true, to_apply=%region_7.8 | all-reduce | flops 80 | bytes 640 | tf_op jit(solution)/shard_map/psum | solution.py:128
  190.4 1.1 fusion.39
  191.7 22.7 %all_gather.3 = bf16[40,256,16]{0,2,1:T(8,128)(2,1)S(1)} all-gather(bf16[40,64,16]{0,2,1:T(8,128)(2,1)S(1)} %copy.206), channel_id=1, replica_groups=mesh['groups'=2,'wide'=4,'narrow'=4] {'wide'}, dimensions={1}, use_global_device_ids=true | all-gather | bytes 409600 | tf_op jit(solution)/shard_map/all_gather | solution.py:138
  214.5 9.5 %fusion = bf16[40,2048]{1,0:T(8,128)(2,1)} fusion(bf16[40,256,16]{0,2,1:T(8,128)(2,1)S(1)} %all_gather.3, bf16[256,16,2048]{2,1,0:T(8,128)(2,1)} %param.30), kind=kOutput, calls=%fused_computation.5 | convolution fusion | flops 671170560 | bytes 17268736 | tf_op jit(solution)/shard_map/rhc,hcd->rd/dot_general | solution.py:136
  224.0 0.7 pad_maximum_fusion.3
  224.7 0.7 pad_maximum_fusion.1
  225.5 17.3 %reduce-scatter.5.cloned.1.call-done = bf16[40,512]{1,0:T(8,128)(2,1)} async-done(((bf16[40,2048]{1,0:T(8,128)(2,1)}), bf16[40,512]{1,0:T(8,128)(2,1)}) %reduce-scatter.5.cloned.1.call-update) | async-done | bytes 40976 | tf_op jit(solution)/shard_map/reduce_scatter | solution.py:142
  242.8 1.4 reshape.330
  (88 shorter events, 7.8 us)
Async XLA Ops:
  7.2 108.1 %copy-start = (bf16[2048,64]{0,1:T(8,128)(2,1)S(1)}, bf16[2048,64]{0,1:T(8,128)(2,1)}, u32[]{:S(2)}) copy-start(bf16[2048,64]{0,1:T(8,128)(2,1)} %param.19) | copy-start | bytes 786436
  7.2 81.0 %copy-start.11 = (bf16[20,2,2048]{2,1,0:T(2,128)(2,1)S(1)}, bf16[20,2,2048]{2,1,0:T(2,128)(2,1)}, u32[]{:S(2)}) copy-start(bf16[20,2,2048]{2,1,0:T(2,128)(2,1)} %param.16) | copy-start | bytes 491524
  7.2 142.4 %reduce-scatter.3.cloned.1.call-start = ((), (), s32[]{:S(2)}) async-start(), calls=%async_computation.2 | async-start | bytes 3276800 | tf_op jit(solution)/shard_map/reduce_scatter | solution.py:80
  88.2 42.8 %copy-start.20 = (bf16[1024]{0:T(1024)(128)(2,1)S(1)}, bf16[1024]{0:T(1024)(128)(2,1)}, u32[]{:S(2)}) copy-start(bf16[1024]{0:T(1024)(128)(2,1)} %param.23) | copy-start | bytes 6148
  88.2 42.8 %copy-start.18 = (bf16[4,1024]{1,0:T(4,128)(2,1)S(1)}, bf16[4,1024]{1,0:T(4,128)(2,1)}, u32[]{:S(2)}) copy-start(bf16[4,1024]{1,0:T(4,128)(2,1)} %param.22) | copy-start | bytes 24580
  88.3 44.6 %copy-start.7 = (bf16[20,3,64,16]{2,3,1,0:T(8,128)(2,1)S(1)}, bf16[20,3,64,16]{2,3,1,0:T(8,128)(2,1)}, u32[]{:S(2)}) copy-start(bf16[20,3,64,16]{2,3,1,0:T(8,128)(2,1)} %param.24) | copy-start | bytes 368644
  88.3 45.9 %copy-start.19 = (bf16[4,64,16]{1,2,0:T(8,128)(2,1)S(1)}, bf16[4,64,16]{1,2,0:T(8,128)(2,1)}, u32[]{:S(2)}) copy-start(bf16[4,64,16]{1,2,0:T(8,128)(2,1)} %param.20) | copy-start | bytes 24580
  112.1 130.7 %reduce-scatter.5.cloned.1.call-start = ((), (), s32[]{:S(2)}) async-start(), calls=%async_computation.3 | async-start | bytes 204800 | tf_op jit(solution)/shard_map/reduce_scatter | solution.py:142
  131.0 0.6 copy-start.9
  150.9 0.7 copy-start.4
  151.6 0.7 copy-start.5
  158.5 21.3 %copy-start.1 = (bf16[20,1,64,16]{3,2,0,1:T(8,128)(2,1)S(1)}, bf16[20,1,64,16]{3,2,0,1:T(8,128)(2,1)}, u32[]{:S(2)}) copy-start(bf16[20,1,64,16]{3,2,0,1:T(8,128)(2,1)} %copy.214) | copy-start | bytes 122884
  158.5 21.3 %copy-start.2 = (bf16[20,1,64,16]{3,2,0,1:T(8,128)(2,1)S(1)}, bf16[20,1,64,16]{3,2,0,1:T(8,128)(2,1)}, u32[]{:S(2)}) copy-start(bf16[20,1,64,16]{3,2,0,1:T(8,128)(2,1)} %copy.217) | copy-start | bytes 122884
  158.5 21.3 %copy-start.3 = (bf16[20,1,64,16]{3,2,0,1:T(8,128)(2,1)S(1)}, bf16[20,1,64,16]{3,2,0,1:T(8,128)(2,1)}, u32[]{:S(2)}) copy-start(bf16[20,1,64,16]{3,2,0,1:T(8,128)(2,1)} %copy.218) | copy-start | bytes 122884
  158.5 21.3 %copy-start.13 = (f32[64,16]{1,0:T(8,128)S(1)}, f32[64,16]{1,0:T(8,128)}, u32[]{:S(2)}) copy-start(f32[64,16]{1,0:T(8,128)} %copy.185) | copy-start | bytes 12292
  158.6 21.3 %copy-start.14 = (f32[64,16]{1,0:T(8,128)S(1)}, f32[64,16]{1,0:T(8,128)}, u32[]{:S(2)}) copy-start(f32[64,16]{1,0:T(8,128)} %copy.183) | copy-start | bytes 12292
  158.6 21.3 %copy-start.15 = (f32[64,16]{1,0:T(8,128)S(1)}, f32[64,16]{1,0:T(8,128)}, u32[]{:S(2)}) copy-start(f32[64,16]{1,0:T(8,128)} %copy.181) | copy-start | bytes 12292
  158.6 21.3 %copy-start.16 = (f32[64,16]{1,0:T(8,128)S(1)}, f32[64,16]{1,0:T(8,128)}, u32[]{:S(2)}) copy-start(f32[64,16]{1,0:T(8,128)} %copy.179) | copy-start | bytes 12292
  158.6 21.3 %copy-start.17 = (f32[64,16]{1,0:T(8,128)S(1)}, f32[64,16]{1,0:T(8,128)}, u32[]{:S(2)}) copy-start(f32[64,16]{1,0:T(8,128)} %copy.178) | copy-start | bytes 12292
  158.6 21.3 %copy-start.21 = (f32[64]{0:T(128)S(1)}, f32[64]{0:T(128)}, u32[]{:S(2)}) copy-start(f32[64]{0:T(128)} %param.28) | copy-start | bytes 772
  181.8 42.2 %copy-start.10 = (bf16[20,2,1024]{2,0,1:T(8,128)(2,1)S(1)}, bf16[20,2,1024]{2,0,1:T(8,128)(2,1)}, u32[]{:S(2)}) copy-start(bf16[20,2,1024]{2,0,1:T(8,128)(2,1)} %copy-done.9) | copy-start | bytes 245764
  181.8 42.2 %copy-start.12 = (bf16[20,3,1024]{2,0,1:T(8,128)(2,1)S(1)}, bf16[20,3,1024]{2,0,1:T(8,128)(2,1)}, u32[]{:S(2)}) copy-start(bf16[20,3,1024]{2,0,1:T(8,128)(2,1)} %param.25) | copy-start | bytes 368644
  181.9 42.8 %copy-start.6 = (bf16[1,40,64,16]{2,3,1,0:T(8,128)(2,1)S(1)}, bf16[1,40,64,16]{2,3,1,0:T(8,128)(2,1)}, u32[]{:S(2)}) copy-start(bf16[1,40,64,16]{2,3,1,0:T(8,128)(2,1)} %copy-done.5) | copy-start | bytes 245764
  181.9 42.8 %copy-start.8 = (bf16[20,3,64,16]{2,3,1,0:T(8,128)(2,1)S(1)}, bf16[20,3,64,16]{2,3,1,0:T(8,128)(2,1)}, u32[]{:S(2)}) copy-start(bf16[20,3,64,16]{2,3,1,0:T(8,128)(2,1)} %param.24) | copy-start | bytes 368644
Sparse Core Ops, SparseCore 0:
  112.2 37.3 reduce-scatter.2
  224.1 18.6 reduce-scatter.4
where the time goes:
time: 254 us; the launch traced here: 251 us
  local copies, waits for them, and re-layouts  104 us (41%)
  blocking collectives  43.9 us (17%)
  matrix products  34.4 us (14%)
  other arithmetic  31.4 us (12%)
  waiting for transfers between devices  22.6 us (9%)
  between operations  14.6 us (6%)
    unnamed x52, local copies, waits for them, and re-layouts  87.9 us
    all_gather x1, blocking collectives, shards(): lax.all_gather(normed, 'wide', axis=1, tiled=True)  22.7 us
    dot_general x1, matrix products, shards(): jnp.einsum('rd,dzhc->czrh', tok_rows, xz_local, preferred_element_type=jn...  21.7 us
    reduce_sum x1, other arithmetic, advance(): jnp.sum(ssm_now * c_tok[:, :, None, :], axis=-1)  21.2 us
    reduce_scatter x1, waiting for transfers between devices, shards(): lax.psum_scatter(out_part.astype(jnp.bfloat16), 'narrow', scatter_dimensi...  17.3 us
    psum x1, blocking collectives, shards(): bc_summed, dt_summed = lax.psum((bc_part, dt_part), 'narrow')  15.5 us
    dot_general x1, matrix products, shards(): jnp.einsum('rhc,hcd->rd', lax.all_gather(normed, 'wide', axis=1, tiled=Tr...  9.51 us
    psum x1, blocking collectives, shards(): group_sum = lax.psum(squares_part, 'narrow')  5.73 us
  transfers between devices with their start and end apart: 2, of which 2 were waited for; matrix products, arithmetic and copies ran while one was open for 7% of the time, Pallas kernels for 0%

commit v1 on v0

v1 whole, which is shorter than its diff:
```python
import functools

import jax
import jax.numpy as jnp
from jax import lax
from jax.experimental import pallas as pl
from jax.experimental.pallas import tpu as pltpu
from jax.sharding import PartitionSpec as P

HEADS = 256
HEAD_DIM = 64
STATE = 256
NGROUPS = 8
LANES = 128
MIB = 2**20

EPSILON = 1e-05

F32 = jnp.float32
BF16 = jnp.bfloat16
VMEM_SPEC = pl.BlockSpec(memory_space=pltpu.VMEM)
SMEM_SPEC = pl.BlockSpec(memory_space=pltpu.SMEM)
ANY_SPEC = pl.BlockSpec(memory_space=pl.ANY)


def exchanged(value, axis, mask):
    return lax.ppermute(value, axis, [(i, i ^ mask) for i in range(lax.axis_size(axis))])


def from_all(value, axis):
    return [value] + [exchanged(value, axis, mask) for mask in range(1, lax.axis_size(axis))]


def silu(value):
    return value / (1.0 + jnp.exp(-value))


def iota(shape, dim):
    return lax.broadcasted_iota(jnp.int32, shape, dim)


def params(mib, **more):
    return pltpu.CompilerParams(vmem_limit_bytes=mib * MIB, **more)


def cost(flops, nbytes):
    return pl.CostEstimate(flops=int(flops), bytes_accessed=int(nbytes), transcendentals=0)


def small_proj_kernel(x_ref, bc_ref, dt_ref, part_ref, spread_ref, *, depth):
    rows, feats = x_ref.shape
    bc_cols = bc_ref.shape[1]
    dt_cols = dt_ref.shape[0]
    part_ref[:, :bc_cols] = jnp.dot(x_ref[...], bc_ref[...], preferred_element_type=F32).astype(BF16)
    dt_part = lax.dot_general(x_ref[...], dt_ref[...], (((1,), (1,)), ((), ())), preferred_element_type=F32)
    pad = jnp.zeros((rows, part_ref.shape[1] - bc_cols - dt_cols), F32)
    part_ref[:, bc_cols:] = jnp.concatenate([dt_part, pad], axis=1).astype(BF16)
    place = iota((depth, 2 * depth), 1) - 2 * iota((depth, 2 * depth), 0)
    for z in range(2):
        one_hot = (place == z).astype(F32).astype(BF16)
        for i in range(feats // depth):
            spread = jnp.dot(x_ref[:, i * depth : (i + 1) * depth], one_hot, preferred_element_type=F32)
            spread_ref[i, z * rows : (z + 1) * rows] = spread.astype(BF16)


def small_proj(x, bc_weight, dt_weight_t, depth):
    rows, feats = x.shape
    bc_cols = bc_weight.shape[1]
    return pl.pallas_call(
        functools.partial(small_proj_kernel, depth=depth),
        out_shape=(
            jax.ShapeDtypeStruct((rows, bc_cols + LANES), BF16),
            jax.ShapeDtypeStruct((feats // depth, 2 * rows, 2 * depth), BF16),
        ),
        in_specs=[VMEM_SPEC] * 3,
        out_specs=(VMEM_SPEC, VMEM_SPEC),
        compiler_params=params(24),
        cost_estimate=cost(2 * rows * feats * (bc_cols + 3 * depth), 2 * feats * bc_cols),
        name="small_proj",
    )(x, bc_weight, dt_weight_t)


def big_proj_kernel(me_ref, x_ref, w_ref, *refs, depth, slots, narrow, chan):
    outs = refs[:narrow]
    wide_tiles, tiles, total, chunks, tile_sem, flat_sem = refs[narrow:]
    steps = w_ref.shape[0] // depth
    blocks = w_ref.shape[1]

    def start(i):
        for block in range(blocks):
            pltpu.make_async_copy(
                w_ref.at[pl.ds(i * depth, depth), block], wide_tiles.at[i % slots, block], tile_sem.at[i % slots]
            ).start()

    def wait(i):
        held = wide_tiles.at[i % slots]
        pltpu.make_async_copy(held, held, tile_sem.at[i % slots]).wait()

    def flat_copy(i):
        source = wide_tiles.at[i % slots].reshape(blocks * 2 * depth, LANES)
        return pltpu.make_async_copy(source, tiles.at[i % 2], flat_sem.at[i % 2])

    for i in range(min(slots, steps)):
        start(i)
    total[...] = jnp.zeros_like(total)
    span = narrow * LANES
    column = iota((span, span), 0)
    target = (column % HEAD_DIM) // chan * LANES + column // HEAD_DIM * chan + column % chan
    mover = (target == iota((span, span), 1)).astype(F32).astype(BF16)
    wait(0)
    flat_copy(0).start()
    for i in range(steps):
        flat_copy(i).wait()
        if i + slots < steps:
            start(i + slots)
        if i + 1 < steps:
            wait(i + 1)
            flat_copy(i + 1).start()
        pair = 2 if blocks % 2 == 0 else 1
        for block in range(0, blocks, pair):
            weight = jnp.concatenate(
                [tiles[i % 2, (block + j) * 2 * depth : (block + j + 1) * 2 * depth] for j in range(pair)], axis=1
            )
            columns = slice(block * LANES, (block + pair) * LANES)
            total[:, columns] += jnp.dot(x_ref[i], weight, preferred_element_type=F32)
    for q in range(total.shape[1] // span):
        moved = jnp.dot(total[:, q * span : (q + 1) * span].astype(BF16), mover, preferred_element_type=F32)
        for n in range(narrow):
            chunks[n, :, q * LANES : (q + 1) * LANES] = moved[:, n * LANES : (n + 1) * LANES].astype(BF16)
    for mask in range(narrow):
        outs[mask][...] = chunks[me_ref[1] ^ mask]


def big_proj(me, spread, weight, depth, narrow, chan):
    feats, _, cols = weight.shape
    rows = spread.shape[1]
    blocks = cols // LANES
    slots = 3
    by_block = weight.reshape(feats, 2, blocks, LANES).transpose(0, 2, 1, 3)
    return pl.pallas_call(
        functools.partial(big_proj_kernel, depth=depth, slots=slots, narrow=narrow, chan=chan),
        out_shape=[jax.ShapeDtypeStruct((rows, cols // narrow), BF16)] * narrow,
        in_specs=[SMEM_SPEC, VMEM_SPEC, ANY_SPEC],
        out_specs=[VMEM_SPEC] * narrow,
        scratch_shapes=[
            pltpu.VMEM((slots, blocks, depth, 2, LANES), BF16),
            pltpu.VMEM((2, blocks * 2 * depth, LANES), BF16),
            pltpu.VMEM((rows, cols), F32),
            pltpu.VMEM((narrow, rows, cols // narrow), BF16),
            pltpu.SemaphoreType.DMA((slots,)),
            pltpu.SemaphoreType.DMA((2,)),
        ],
        compiler_params=params(32),
        cost_estimate=cost(2 * rows * feats * 2 * cols, 4 * feats * cols),
        name="big_proj",
    )(me, spread, by_block)


def conv_pair(history, fresh, taps, offset):
    window = list(history) + list(fresh)
    outputs = []
    for token in range(2):
        summed = offset
        for tap in range(4):
            summed = summed + taps[tap : tap + 1] * window[token + tap]
        outputs.append(silu(summed))
    return outputs


def bc_conv_kernel(*refs, parts, seqs):
    part_refs = refs[:parts]
    history_ref, taps_ref, offset_ref, conv_ref, kept_ref, dt_ref = refs[parts:]
    summed = part_refs[0][...].astype(F32)
    for part_ref in part_refs[1:]:
        summed = summed + part_ref[...].astype(F32)
    half = summed.shape[0] // 2
    cols = taps_ref.shape[1]
    proj = summed.astype(BF16).astype(F32)
    dt_ref[...] = proj[:, cols:]
    fresh = [proj[:seqs, :cols], proj[half : half + seqs, :cols]]
    history = [history_ref[i].astype(F32) for i in range(3)]
    conv_ref[...] = jnp.zeros_like(conv_ref)
    for token, value in enumerate(conv_pair(history, fresh, taps_ref[...].astype(F32), offset_ref[...].astype(F32))):
        conv_ref[token * half : token * half + seqs] = value
    kept_ref[0] = history_ref[2]
    kept_ref[1] = fresh[0].astype(BF16)
    kept_ref[2] = fresh[1].astype(BF16)


def bc_conv(parts, history, taps, offset):
    rows = parts[0].shape[0]
    cols = taps.shape[1]
    return pl.pallas_call(
        functools.partial(bc_conv_kernel, parts=len(parts), seqs=history.shape[1]),
        out_shape=(
            jax.ShapeDtypeStruct((rows, cols), F32),
            jax.ShapeDtypeStruct(history.shape, BF16),
            jax.ShapeDtypeStruct((rows, LANES), F32),
        ),
        in_specs=[VMEM_SPEC] * (len(parts) + 3),
        out_specs=(VMEM_SPEC,) * 3,
        compiler_params=params(8),
        cost_estimate=cost(30 * rows * cols, 8 * rows * cols),
        name="bc_conv",
    )(*parts, history, taps, offset)


def state_read_kernel(bc_ref, state_ref, read_ref, *, groups):
    step = pl.program_id(0)
    count, rows, _ = state_ref.shape
    half = bc_ref.shape[0] // 2
    span = rows // groups

    @pl.when(step == 0)
    def _():
        read_ref[...] = jnp.zeros_like(read_ref)

    for j in range(count):
        seq = step * count + j
        for g in range(groups):
            cols = slice((2 * g + 1) * STATE, (2 * g + 2) * STATE)
            both = jnp.concatenate([bc_ref[pl.ds(t * half + seq, 1), cols] for t in range(2)], axis=0)
            held = state_ref[j, g * span : (g + 1) * span].astype(BF16)
            out = lax.dot_general(both.astype(BF16), held, (((1,), (1,)), ((), ())), preferred_element_type=F32)
            for t in range(2):
                read_ref[pl.ds(t * half + seq, 1), g * span : (g + 1) * span] = out[t : t + 1]


def state_read(bc, state, groups, count):
    seqs, rows, _ = state.shape
    return pl.pallas_call(
        functools.partial(state_read_kernel, groups=groups),
        grid=(seqs // count,),
        out_shape=jax.ShapeDtypeStruct((bc.shape[0], rows), F32),
        in_specs=[
            pl.BlockSpec(bc.shape, lambda i: (0, 0)),
            pl.BlockSpec((count, rows, STATE), lambda i: (i, 0, 0)),
        ],
        out_specs=pl.BlockSpec((bc.shape[0], rows), lambda i: (0, 0)),
        compiler_params=params(16),
        cost_estimate=cost(4 * state.size, 4 * state.size),
        name="state_read",
    )(bc, state)


def readout_kernel(*refs, parts, seqs, groups, heads, chan):
    part_refs = refs[:parts]
    history_ref, small_ref, offset_ref, gain_ref, read_ref, bc_ref, dt_ref, heads_ref = refs[parts : parts + 8]
    sent_ref, fresh_ref, scale_ref, decay_ref = refs[parts + 8 :]
    summed = part_refs[0][...].astype(F32)
    for part_ref in part_refs[1:]:
        summed = summed + part_ref[...].astype(F32)
    proj = summed.astype(BF16).astype(F32)
    half = proj.shape[0] // 4
    width = proj.shape[1]
    gates = [proj[:half], proj[half : 2 * half]]
    fresh = [proj[2 * half : 3 * half], proj[3 * half :]]
    fresh_ref[...] = proj[2 * half :].astype(BF16)
    history = [history_ref[i * half : (i + 1) * half].astype(F32) for i in range(3)]
    x = conv_pair(history, fresh, small_ref[...].astype(F32), offset_ref[...].astype(F32))

    bias, rate, skip = heads_ref[0:1], jnp.exp(heads_ref[1:2]), heads_ref[2:3]
    raw = dt_ref[:, :heads] + bias
    step = jnp.maximum(raw, 0.0) + jnp.log1p(jnp.exp(-jnp.abs(raw)))
    decay = jnp.exp(-step * rate)
    decay_ref[...] = decay[:half] * decay[half:]
    repeat = (iota((heads, width), 1) // chan == iota((heads, width), 0)).astype(F32)
    packed = jnp.concatenate([step, decay, jnp.broadcast_to(skip, (8, heads))], axis=0)
    spread = jnp.dot(packed, repeat, preferred_element_type=F32, precision=lax.Precision.HIGHEST)
    steps = [spread[:half], spread[half : 2 * half]]
    decays = [spread[2 * half : 3 * half], spread[3 * half : 4 * half]]
    skips = spread[4 * half : 4 * half + 1]

    span = width // groups

    def dots(b_token, c_token):
        out = []
        for g in range(groups):
            b = bc_ref[b_token * half : (b_token + 1) * half, 2 * g * STATE : (2 * g + 1) * STATE]
            c = bc_ref[c_token * half : (c_token + 1) * half, (2 * g + 1) * STATE : (2 * g + 2) * STATE]
            out.append(jnp.broadcast_to(jnp.sum(b * c, axis=1, keepdims=True), (half, span)))
        return jnp.concatenate(out, axis=1)

    first = steps[0] * x[0]
    second = steps[1] * x[1]
    carried = decays[1] * first
    y = [
        decays[0] * read_ref[:half] + first * dots(0, 0) + skips * x[0],
        decays[0] * decays[1] * read_ref[half:] + carried * dots(0, 1) + second * dots(1, 1) + skips * x[1],
    ]
    scale_ref[:half] = carried
    scale_ref[half:] = second
    gain = gain_ref[...].astype(F32)
    lane = iota((half, LANES), 1)
    for token in range(2):
        gated = y[token] * silu(gates[token])
        rows = slice(token * half, (token + 1) * half)
        sent_ref[rows, :width] = (gated * gain).astype(BF16)
        squares = jnp.zeros((half, LANES), F32)
        for g in range(groups):
            part = gated[:, g * span : (g + 1) * span]
            total = jnp.sum(part * part, axis=1, keepdims=True)
            high = total.astype(BF16).astype(F32)
            squares = squares + jnp.where(lane == 2 * g, high, 0.0) + jnp.where(lane == 2 * g + 1, total - high, 0.0)
        sent_ref[rows, width:] = squares.astype(BF16)


def readout(parts, history, taps, offset, gain, read, bc, dt, head_vals, seqs, groups, chan):
    rows, width = read.shape
    heads = head_vals.shape[1]
    return pl.pallas_call(
        functools.partial(readout_kernel, parts=len(parts), seqs=seqs, groups=groups, heads=heads, chan=chan),
        out_shape=(
            jax.ShapeDtypeStruct((rows, width + LANES), BF16),
            jax.ShapeDtypeStruct((rows, width), BF16),
            jax.ShapeDtypeStruct((rows, width), F32),
            jax.ShapeDtypeStruct((rows // 2, heads), F32),
        ),
        in_specs=[VMEM_SPEC] * (len(parts) + 8),
        out_specs=(VMEM_SPEC,) * 4,
        compiler_params=params(16),
        cost_estimate=cost(100 * rows * width, 12 * rows * width),
        name="readout",
    )(*parts, history, taps, offset, gain, read, bc, dt, head_vals)


def state_write_kernel(scale_ref, decay_ref, bc_ref, state_ref, *refs, groups, first):
    new_ref, left, decays = refs[-3:]
    step = pl.program_id(0)
    count, rows, _ = state_ref.shape
    half = bc_ref.shape[0] // 2
    span = rows // groups
    heads = decay_ref.shape[1]
    chan = rows // heads
    seqs = decays.shape[0] // heads

    @pl.when(step == 0)
    def _():
        scale = scale_ref[...]
        high = scale.astype(BF16).astype(F32)
        pad = jnp.zeros((left.shape[1] - 6 * half, rows), F32)
        left[...] = jnp.concatenate([high, scale - high, high, pad], axis=0).T.astype(BF16)
        by_head = decay_ref[...].T
        for s in range(seqs):
            decays[s * heads : (s + 1) * heads] = jnp.broadcast_to(by_head[:, s : s + 1], (heads, LANES))

    row = iota((left.shape[1], STATE), 0)
    for j in range(count):
        seq = (step + first) * count + j
        for g in range(groups):
            b = [bc_ref[pl.ds(t * half + seq, 1), 2 * g * STATE : (2 * g + 1) * STATE] for t in range(2)]
            high = [value.astype(BF16).astype(F32) for value in b]
            low = [value - top for value, top in zip(b, high)]
            right = jnp.zeros(row.shape, F32)
            for block, value in enumerate(high + high + low):
                right = jnp.where(row == block * half + seq, value, right)
            here = slice(g * span, (g + 1) * span)
            added = jnp.dot(left[here], right.astype(BF16), preferred_element_type=F32)
            for h in range(span // chan):
                head = g * (span // chan) + h
                decay = decays[pl.ds(seq * heads + head, 1), :]
                decay = jnp.concatenate([decay] * (STATE // LANES), axis=1)
                new_ref[j, head * chan : (head + 1) * chan] = (
                    decay * state_ref[j, head * chan : (head + 1) * chan] + added[h * chan : (h + 1) * chan]
                )


def state_write(scale, decay, bc, state, groups, count, first, steps, before=None):
    seqs, rows, _ = state.shape
    half = bc.shape[0] // 2
    heads = decay.shape[1]
    depth = -(-6 * half // LANES) * LANES
    whole = lambda array: pl.BlockSpec(array.shape, lambda i: (0, 0))
    block = pl.BlockSpec((count, rows, STATE), lambda i: (i + first, 0, 0))
    extra = [] if before is None else [before]
    return pl.pallas_call(
        functools.partial(state_write_kernel, groups=groups, first=first),
        grid=(steps,),
        out_shape=jax.ShapeDtypeStruct(state.shape, F32),
        in_specs=[whole(scale), whole(decay), whole(bc), block] + [ANY_SPEC] * len(extra),
        out_specs=block,
        scratch_shapes=[pltpu.VMEM((rows, depth), BF16), pltpu.VMEM((seqs * heads, LANES), F32)],
        input_output_aliases={4: 0} if extra else {},
        compiler_params=params(24),
        cost_estimate=cost(4 * count * steps * rows * STATE, 8 * count * steps * rows * STATE),
        name="state_write",
    )(scale, decay, bc, state, *extra)


def out_proj_kernel(me_ref, *refs, wide, narrow, groups, group_span):
    sent = refs[:wide]
    squares = refs[wide : wide + narrow]
    w_ref = refs[wide + narrow]
    outs = refs[wide + narrow + 1 : wide + 2 * narrow + 1]
    total, chunks = refs[wide + 2 * narrow + 1 :]
    summed = squares[0][...]
    for ref in squares[1:]:
        summed = summed + ref[...]
    rows = total.shape[0]
    width = w_ref.shape[0] // wide
    span = width // groups
    lane = iota(summed.shape, 1)
    for mask in range(wide):
        owner = me_ref[0] ^ mask
        scaled = []
        for g in range(groups):
            low = (owner // group_span * group_span) * groups + g
            mine = (lane >= low) & (lane < low + (group_span - 1) * groups + 1)
            group_sum = jnp.sum(jnp.where(mine, summed, 0.0), axis=1, keepdims=True)
            inverse = lax.rsqrt(group_sum / (HEADS // NGROUPS * HEAD_DIM) + EPSILON)
            scaled.append(sent[mask][:, g * span : (g + 1) * span].astype(F32) * inverse)
        normed = jnp.concatenate(scaled, axis=1).astype(BF16)
        weight = w_ref[pl.ds(pl.multiple_of(owner * width, width), width), :]
        product = jnp.dot(normed, weight, preferred_element_type=F32)
        total[...] = product if mask == 0 else total[...] + product
    cols = total.shape[1] // narrow
    for n in range(narrow):
        chunks[n] = total[:, n * cols : (n + 1) * cols].astype(BF16)
    for mask in range(narrow):
        outs[mask][...] = chunks[me_ref[1] ^ mask]


def out_proj(me, sent, squares, weight, groups, group_span):
    wide, narrow = len(sent), len(squares)
    rows = sent[0].shape[0]
    depth, cols = weight.shape
    return pl.pallas_call(
        functools.partial(out_proj_kernel, wide=wide, narrow=narrow, groups=groups, group_span=group_span),
        out_shape=[jax.ShapeDtypeStruct((rows, cols // narrow), BF16)] * narrow,
        in_specs=[SMEM_SPEC] + [VMEM_SPEC] * (wide + narrow + 1),
        out_specs=[VMEM_SPEC] * narrow,
        scratch_shapes=[pltpu.VMEM((rows, cols), F32), pltpu.VMEM((narrow, rows, cols // narrow), BF16)],
        compiler_params=params(28),
        cost_estimate=cost(2 * rows * depth * cols, 2 * depth * cols),
        name="out_proj",
    )(me, *sent, *squares, weight)


def shards(
    inputs,
    xz_weight,
    bc_weight,
    dt_weight,
    conv_x_weight,
    conv_x_bias,
    conv_bc_weight,
    conv_bc_bias,
    conv_x_state,
    conv_bc_state,
    dt_bias,
    a_log,
    d_skip,
    norm_weight,
    out_weight,
    ssm_state,
):
    seqs = inputs.shape[0]
    feats = inputs.shape[2]
    heads = dt_weight.shape[1]
    wide = lax.axis_size("wide")
    narrow = lax.axis_size("narrow")
    chan = HEAD_DIM // narrow
    width = heads * chan
    half = -(-seqs // 8) * 8
    groups = max(NGROUPS // wide, 1)
    group_span = max(wide // NGROUPS, 1)
    depth = min(256, feats)
    me = jnp.stack([lax.axis_index("wide"), lax.axis_index("narrow")]).astype(jnp.int32)

    def rows_of(value):
        padded = jnp.pad(value, ((0, 0), (0, half - seqs), (0, 0)))
        return padded.reshape(value.shape[0] * half, value.shape[2])

    x = rows_of(inputs.transpose(1, 0, 2))
    part, spread = small_proj(x, bc_weight, dt_weight.T, depth)
    bc_parts = from_all(part, "narrow")
    chunks = big_proj(me, spread, xz_weight, depth, narrow, chan)

    conv, kept_bc, dt = bc_conv(
        bc_parts, conv_bc_state.transpose(1, 0, 2), conv_bc_weight, conv_bc_bias.reshape(1, -1)
    )
    for bit in range(group_span.bit_length() - 1):
        partner = exchanged(conv.astype(BF16), "wide", 1 << bit).astype(F32)
        is_lower = lax.axis_index("wide") // (1 << bit) % 2 == 0
        conv = jnp.where(
            is_lower, jnp.concatenate([conv, partner], axis=1), jnp.concatenate([partner, conv], axis=1)
        )

    xz_parts = [chunks[0]] + [exchanged(chunks[mask], "narrow", mask) for mask in range(1, narrow)]
    state = ssm_state.reshape(seqs, width, STATE)
    count = 2 if seqs % 2 == 0 else 1
    read = state_read(conv, state, groups, count)

    history = rows_of(conv_x_state.reshape(seqs, 3, width).transpose(1, 0, 2))
    sent, fresh, scale, decay = readout(
        xz_parts,
        history,
        conv_x_weight.reshape(-1, width),
        conv_x_bias.reshape(1, width),
        norm_weight.reshape(1, width),
        read,
        conv,
        dt,
        jnp.stack([dt_bias, a_log, d_skip]),
        seqs,
        groups,
        chan,
    )

    gathered = from_all(sent, "wide")
    steps = seqs // count
    early = steps // 2
    new_state = state_write(scale, decay, conv, state, groups, count, 0, early)
    square_parts = [value[:, width:].astype(F32) for value in gathered]
    square_parts = [
        sum(value[:, 2 * g : 2 * g + 2].sum(axis=1, keepdims=True) for value in [piece])
        for piece in square_parts
        for g in range(groups)
    ]
    wide_index = lax.axis_index("wide")
    lane = jnp.arange(LANES)[None, :]
    squares = jnp.zeros((sent.shape[0], LANES), F32)
    for mask in range(wide):
        for g in range(groups):
            place = (wide_index ^ mask) * groups + g
            squares = squares + jnp.where(lane == place, square_parts[mask * groups + g], 0.0)
    square_list = from_all(squares, "narrow")
    new_state = state_write(scale, decay, conv, state, groups, count, early, steps - early, new_state)

    out_chunks = out_proj(me, gathered, square_list, out_weight.reshape(-1, out_weight.shape[2]), groups, group_span)
    out_sum = out_chunks[0].astype(F32)
    for mask in range(1, narrow):
        out_sum = out_sum + exchanged(out_chunks[mask], "narrow", mask).astype(F32)
    layer_out = out_sum.astype(BF16).reshape(2, half, -1)[:, :seqs].transpose(1, 0, 2)

    fresh = fresh.reshape(2, half, heads, chan)[:, :seqs].transpose(1, 0, 2, 3)
    new_conv_x = jnp.concatenate([conv_x_state[:, 2:], fresh], axis=1)
    return (layer_out, new_state.reshape(ssm_state.shape), new_conv_x, kept_bc.transpose(1, 0, 2))


def solution(mesh):
    return jax.shard_map(
        shards,
        mesh=mesh,
        in_specs=(
            P("groups", None, "narrow"),
            P("narrow", None, "wide"),
            P("narrow", "wide"),
            P("narrow", "wide"),
            P(None, "wide", "narrow"),
            P("wide", "narrow"),
            P(None, "wide"),
            P("wide"),
            P("groups", None, "wide", "narrow"),
            P("groups", None, "wide"),
            P("wide"),
            P("wide"),
            P("wide"),
            P("wide", "narrow"),
            P(None, "narrow", "wide"),
            P("groups", "wide", "narrow", None),
        ),
        out_specs=(
            P("groups", None, ("wide", "narrow")),
            P("groups", "wide", "narrow", None),
            P("groups", None, "wide", "narrow"),
            P("groups", None, "wide"),
        ),
        check_vma=False,
    )
```

time: 254 us -> 104 us (0.41); the launches traced: 251 us -> 104 us
  local copies, waits for them, and re-layouts: 104 us -> 28.9 us
  blocking collectives: 43.9 us -> 0 us
  Pallas kernels: 0 us -> 41.5 us
  matrix products: 34.4 us -> 0 us
  other arithmetic: 31.4 us -> 1.72 us
  starting transfers between devices: 0.08 us -> 13.7 us
  between operations: 14.6 us -> 0.99 us
  waiting for transfers between devices: 22.6 us -> 17.2 us
    unnamed x52 -> x36, local copies, waits for them, and re-layouts: 87.9 us -> 25.3 us
    pallas_call x0 -> x8, Pallas kernels: none -> 41.5 us  [the longest x1 18.1 us: big_proj(): pl.pallas_call(functools.partial(big_proj_kernel, depth=depth, slots=slot...]
    dot_general x4 -> x0, matrix products: 34.4 us -> none  [the longest x1 21.7 us: shards(): jnp.einsum('rd,dzhc->czrh', tok_rows, xz_local, preferred_element_type=jn...]
    all_gather x1 -> x0, blocking collectives: 22.7 us -> none  [shards(): lax.all_gather(normed, 'wide', axis=1, tiled=True)]
    reduce_scatter x2 -> x0, waiting for transfers between devices: 22.6 us -> none  [the longest x1 17.3 us: shards(): lax.psum_scatter(out_part.astype(jnp.bfloat16), 'narrow', scatter_dimensi...]
    reduce_sum x3 -> x4, other arithmetic: 22.4 us -> 0.69 us  [shards(): value[:, 2 * g:2 * g + 2].sum(axis=1, keepdims=True)]
    psum x2 -> x0, blocking collectives: 21.2 us -> none  [the longest x1 15.5 us: shards(): bc_summed, dt_summed = lax.psum((bc_part, dt_part), 'narrow')]
    ppermute x0 -> x15, waiting for transfers between devices: none -> 17.2 us  [exchanged(): lax.ppermute(value, axis, [(i, i ^ mask) for i in range(lax.axis_size(axi...]
  transfers between devices with their start and end apart: 2 -> 15, of which waited for: 2 -> 4; matrix products, arithmetic and copies ran while one was open for 7% -> 6% of each run, Pallas kernels for 0% -> 34%
where the time goes in v1:
time: 104 us
  Pallas kernels  41.5 us (40%)
  local copies, waits for them, and re-layouts  28.9 us (28%)
  waiting for transfers between devices  17.2 us (17%)
  starting transfers between devices  13.7 us (13%)
  other arithmetic  1.72 us (2%)
    unnamed x36, local copies, waits for them, and re-layouts  25.3 us
    pallas_call x1, Pallas kernels, big_proj(): pl.pallas_call(functools.partial(big_proj_kernel, depth=depth, slots=slot...  18.1 us
    ppermute x15, waiting for transfers between devices, exchanged(): lax.ppermute(value, axis, [(i, i ^ mask) for i in range(lax.axis_size(axi...  17.2 us
    ppermute x15, starting transfers between devices, exchanged(): lax.ppermute(value, axis, [(i, i ^ mask) for i in range(lax.axis_size(axi...  13.7 us
    pallas_call x2, Pallas kernels, state_write(): pl.pallas_call(functools.partial(state_write_kernel, groups=groups, first...  12.7 us
    pallas_call x1, Pallas kernels, state_read(): pl.pallas_call(functools.partial(state_read_kernel, groups=groups), grid=...  3.96 us
    pallas_call x1, Pallas kernels, out_proj(): pl.pallas_call(functools.partial(out_proj_kernel, wide=wide, narrow=narro...  3.67 us
  transfers between devices with their start and end apart: 15, of which 4 were waited for; matrix products, arithmetic and copies ran while one was open for 6% of the time, Pallas kernels for 34%

profile of v1, /device:TPU:0, one launch (start us, length us, event | category | flops | bytes accessed | tf_op | source)
XLA Modules:
  0.0 104.1 jit_solution(5751846917881493106)
XLA Ops:
  0.6 1.0 copy.45
  1.7 2.2 %copy-done.3 = bf16[2048,1024]{1,0:T(8,128)(2,1)S(1)} copy-done((bf16[2048,1024]{1,0:T(8,128)(2,1)S(1)}, bf16[2048,1024]{1,0:T(8,128)(2,1)}, u32[]{:S(2)}) %copy-start.3) | copy-done | bytes 4194328
  3.9 0.9 copy-done.4
  4.9 1.6 %small_proj.1 = (bf16[48,1152]{1,0:T(8,128)(2,1)S(1)}, bf16[8,96,512]{2,1,0:T(8,128)(2,1)S(1)}) custom-call(bf16[48,2048]{1,0:T(8,128)(2,1)S(1)} %bitcast.35, bf16[2048,1024]{1,0:T(8,128)(2,1)S(1)} %copy-done.3, bf16[64,2048]{1,0:T(8,128)(2,1)S(1)} %bitcast.37), custom_call_target="tpu_custom_call" | custom-call | flops 352321536 | bytes 4194304 | tf_op jit(solution)/shard_map/small_proj/pallas_call | solution.py:69
  6.5 0.5 collective-permute-start.3
  7.1 2.6 %collective-permute-start.4 = (bf16[48,1152]{1,0:T(8,128)(2,1)S(1)}, bf16[48,1152]{1,0:T(8,128)(2,1)S(1)}, u32[]{:S(2)}, u32[]{:S(2)}) collective-permute-start(bf16[48,1152]{1,0:T(8,128)(2,1)S(1)} %get-tuple-element.26.refs_0_), channel_id=1, source_target_pairs={{0,2},{1,3},{2,0},{3,1},{4,6},{5,7},{6,4},{7,5},{8,10},{9,11},{10,... | collective-permute-start | bytes 331784 | tf_op jit(solution)/shard_map/ppermute | solution.py:27
  9.7 18.1 %big_proj.1 = (bf16[96,1024]{1,0:T(8,128)(2,1)S(1)}, bf16[96,1024]{1,0:T(8,128)(2,1)S(1)}, bf16[96,1024]{1,0:T(8,128)(2,1)S(1)}, bf16[96,1024]{1,0:T(8,128)(2,1)S(1)}) custom-call(s32[2]{0:T(128)S(1)} %pad_add_fusion.me_ref, bf16[8,96,512]{2,1,0:T(8,128)(2,1)S(1)} %get-tuple-element.21.x_ref, bf16[2048,32,2,128]{3,2,1,0:T(2,128)(2,1)} %bitcast.40), custom_call_target="tpu_custom_call" | custom-call | flops 3221225472 | bytes 33554432 | tf_op jit(solution)/shard_map/big_proj/pallas_call | solution.py:140
  28.3 1.4 %collective-permute-start.2 = (bf16[96,1024]{1,0:T(8,128)(2,1)S(1)}, bf16[96,1024]{1,0:T(8,128)(2,1)S(1)}, u32[]{:S(2)}, u32[]{:S(2)}) collective-permute-start(bf16[96,1024]{1,0:T(8,128)(2,1)S(1)} %get-tuple-element.25), channel_id=1, source_target_pairs={{0,3},{1,2},{2,1},{3,0},{4,7},{5,6},{6,5},{7,4},{8,11},{9,10},{10,... | collective-permute-start | bytes 589832 | tf_op jit(solution)/shard_map/ppermute | solution.py:27
  29.7 0.4 copy.37
  30.2 1.6 %reshape.97 = bf16[20,3,1024]{2,0,1:T(8,128)(2,1)S(1)} reshape(bf16[20,3,64,16]{3,2,0,1:T(8,128)(2,1)S(1)} %copy.37) | data formatting | bytes 245760 | tf_op jit(solution)/shard_map/reshape | solution.py:494
  33.0 8.2 %collective-permute-done.5.refs_3_ = bf16[48,1152]{1,0:T(8,128)(2,1)S(1)} collective-permute-done((bf16[48,1152]{1,0:T(8,128)(2,1)S(1)}, bf16[48,1152]{1,0:T(8,128)(2,1)S(1)}, u32[]{:S(2)}, u32[]{:S(2)}) %collective-permute-start.5) | collective-permute-done | bytes 110624 | tf_op jit(solution)/shard_map/ppermute | solution.py:27
  41.2 0.8 bc_conv.1
  42.0 7.0 %copy-done = f32[20,64,16,256]{3,2,1,0:T(8,128)S(1)} copy-done((f32[20,64,16,256]{3,2,1,0:T(8,128)S(1)}, f32[20,64,16,256]{3,2,1,0:T(8,128)}, u32[]{:S(2)}) %copy-start) | copy-done | bytes 20971544
  48.9 4.0 %state_read.1.refs_8_ = f32[48,1024]{1,0:T(8,128)S(1)} custom-call(f32[48,1024]{1,0:T(8,128)S(1)} %get-tuple-element.27.bc_ref.refs_9_, f32[20,1024,256]{2,1,0:T(8,128)S(1)} %bitcast.31), custom_call_target="tpu_custom_call" | custom-call | flops 20971520 | bytes 20971520 | tf_op jit(solution)/shard_map/state_read/pallas_call | solution.py:231
  52.9 0.7 readout.1
  53.6 1.7 %collective-permute-start.6 = (bf16[48,1152]{1,0:T(8,128)(2,1)S(1)}, bf16[48,1152]{1,0:T(8,128)(2,1)S(1)}, u32[]{:S(2)}, u32[]{:S(2)}) collective-permute-start(bf16[48,1152]{1,0:T(8,128)(2,1)S(1)} %get-tuple-element.29.refs_0_), channel_id=1, source_target_pairs={{0,4},{4,0},{8,12},{12,8},{1,5},{5,1},{9,13},{13,9},{2,6},{6,2},{1... | collective-permute-start | bytes 331784 | tf_op jit(solution)/shard_map/ppermute | solution.py:27
  55.3 2.6 %collective-permute-start.7 = (bf16[48,1152]{1,0:T(8,128)(2,1)S(1)}, bf16[48,1152]{1,0:T(8,128)(2,1)S(1)}, u32[]{:S(2)}, u32[]{:S(2)}) collective-permute-start(bf16[48,1152]{1,0:T(8,128)(2,1)S(1)} %get-tuple-element.29.refs_0_), channel_id=1, source_target_pairs={{0,8},{4,12},{8,0},{12,4},{1,9},{5,13},{9,1},{13,5},{2,10},{6,14},... | collective-permute-start | bytes 331784 | tf_op jit(solution)/shard_map/ppermute | solution.py:27
  58.7 7.2 %collective-permute-done.8.refs_3_ = bf16[48,1152]{1,0:T(8,128)(2,1)S(1)} collective-permute-done((bf16[48,1152]{1,0:T(8,128)(2,1)S(1)}, bf16[48,1152]{1,0:T(8,128)(2,1)S(1)}, u32[]{:S(2)}, u32[]{:S(2)}) %collective-permute-start.8) | collective-permute-done | bytes 110624 | tf_op jit(solution)/shard_map/ppermute | solution.py:27
  66.1 0.8 collective-permute-done.7.refs_2_
  67.5 0.6 collective-permute-start.10
  68.1 1.3 %collective-permute-start.11 = (f32[48,128]{1,0:T(8,128)S(1)}, f32[48,128]{1,0:T(8,128)S(1)}, u32[]{:S(2)}, u32[]{:S(2)}) collective-permute-start(f32[48,128]{1,0:T(8,128)S(1)} %select_add_fusion.refs_4_), channel_id=1, source_target_pairs={{0,3},{1,2},{2,1},{3,0},{4,7},{5,6},{6,5},{7,4},{8,11},{9,10},{10,... | collective-permute-start | bytes 73736 | tf_op jit(solution)/shard_map/ppermute | solution.py:27
  69.7 0.9 copy.43
  70.6 1.0 collective-permute-done.10.refs_6_
  71.6 5.8 %copy-done.2 = bf16[256,16,2048]{2,1,0:T(8,128)(2,1)S(1)} copy-done((bf16[256,16,2048]{2,1,0:T(8,128)(2,1)S(1)}, bf16[256,16,2048]{2,1,0:T(8,128)(2,1)}, u32[]{:S(2)}) %copy-start.2) | copy-done | bytes 16777240
  77.3 3.7 %out_proj.1 = (bf16[48,512]{1,0:T(8,128)(2,1)S(1)}, bf16[48,512]{1,0:T(8,128)(2,1)S(1)}, bf16[48,512]{1,0:T(8,128)(2,1)S(1)}, bf16[48,512]{1,0:T(8,128)(2,1)S(1)}) custom-call(s32[2]{0:T(128)S(1)} %pad_add_fusion.me_ref, bf16[48,1152]{1,0:T(8,128)(2,1)S(1)} %get-tuple-element.29.refs_0_, bf16[48,1152]{1,0:T(8,128)(2,1)S(1)} %collective-permute-done.6.refs_1_, ...), custom_call_target="tpu_custom_call" | custom-call | flops 805306368 | bytes 16777216 | tf_op jit(solution)/shard_map/out_proj/pallas_call | solution.py:427
  81.0 1.1 %collective-permute-start.14 = (bf16[48,512]{1,0:T(8,128)(2,1)S(1)}, bf16[48,512]{1,0:T(8,128)(2,1)S(1)}, u32[]{:S(2)}, u32[]{:S(2)}) collective-permute-start(bf16[48,512]{1,0:T(8,128)(2,1)S(1)} %get-tuple-element.33), channel_id=1, source_target_pairs={{0,3},{1,2},{2,1},{3,0},{4,7},{5,6},{6,5},{7,4},{8,11},{9,10},{10,... | collective-permute-start | bytes 147464 | tf_op jit(solution)/shard_map/ppermute | solution.py:27
  82.1 0.7 collective-permute-start.13
  83.0 0.7 pad_maximum_fusion
  83.7 7.0 %copy-done.1 = f32[20,64,16,256]{3,2,1,0:T(8,128)S(1)} copy-done((f32[20,64,16,256]{3,2,1,0:T(8,128)S(1)}, f32[20,64,16,256]{3,2,1,0:T(8,128)}, u32[]{:S(2)}) %copy-start.1) | copy-done | bytes 20971544
  90.7 6.4 %state_write.2.refs_0_ = f32[20,1024,256]{2,1,0:T(8,128)} custom-call(f32[48,1024]{1,0:T(8,128)S(1)} %get-tuple-element.34.scale_ref, f32[24,64]{1,0:T(8,128)S(1)} %get-tuple-element.35.decay_ref, f32[48,1024]{1,0:T(8,128)S(1)} %get-tuple-element.27.bc_ref.refs_9_, f32[20,1024,256]{2,1,0:T(8,128)S(1)} %bitcast.32), custom_call_target="tpu_custom_call" | custom-call | flops 10485760 | bytes 20971520 | tf_op jit(solution)/shard_map/state_write/pallas_call | solution.py:376
  97.0 6.3 %state_write.3 = f32[20,1024,256]{2,1,0:T(8,128)} custom-call(f32[48,1024]{1,0:T(8,128)S(1)} %get-tuple-element.34.scale_ref, f32[24,64]{1,0:T(8,128)S(1)} %get-tuple-element.35.decay_ref, f32[48,1024]{1,0:T(8,128)S(1)} %get-tuple-element.27.bc_ref.refs_9_, f32[20,1024,256]{2,1,0:T(8,128)S(1)} %bitcast.33, ...), custom_call_target="tpu_custom_call", output_to_operand_aliasing={{}: (4, {})} | custom-call | flops 10485760 | bytes 20971520 | tf_op jit(solution)/shard_map/state_write/pallas_call | solution.py:376
  103.4 0.6 copy.47
  (72 shorter events, 3.8 us)
Async XLA Ops:
  0.6 29.1 %copy-start.7 = (bf16[20,3,64,16]{2,3,1,0:T(8,128)(2,1)S(1)}, bf16[20,3,64,16]{2,3,1,0:T(8,128)(2,1)}, u32[]{:S(2)}) copy-start(bf16[20,3,64,16]{2,3,1,0:T(8,128)(2,1)} %param.24) | copy-start | bytes 368644
  1.7 30.2 %copy-start.8 = (bf16[4,64,16]{1,2,0:T(8,128)(2,1)S(1)}, bf16[4,64,16]{1,2,0:T(8,128)(2,1)}, u32[]{:S(2)}) copy-start(bf16[4,64,16]{1,2,0:T(8,128)(2,1)} %param.20) | copy-start | bytes 24580
  1.7 2.2 %copy-start.3 = (bf16[2048,1024]{1,0:T(8,128)(2,1)S(1)}, bf16[2048,1024]{1,0:T(8,128)(2,1)}, u32[]{:S(2)}) copy-start(bf16[2048,1024]{1,0:T(8,128)(2,1)} %bc_ref.1) | copy-start | bytes 12582916
  3.9 0.9 copy-start.4
  4.8 27.2 %copy-start.9 = (bf16[64,16]{0,1:T(8,128)(2,1)S(1)}, bf16[64,16]{0,1:T(8,128)(2,1)}, u32[]{:S(2)}) copy-start(bf16[64,16]{0,1:T(8,128)(2,1)} %param.21) | copy-start | bytes 6148
  4.8 27.4 %copy-start.10 = (bf16[64,16]{0,1:T(8,128)(2,1)S(1)}, bf16[64,16]{0,1:T(8,128)(2,1)}, u32[]{:S(2)}) copy-start(bf16[64,16]{0,1:T(8,128)(2,1)} %param.29) | copy-start | bytes 6148
  4.8 27.6 %copy-start.11 = (bf16[1024]{0:T(1024)(128)(2,1)S(1)}, bf16[1024]{0:T(1024)(128)(2,1)}, u32[]{:S(2)}) copy-start(bf16[1024]{0:T(1024)(128)(2,1)} %param.23) | copy-start | bytes 6148
  4.8 27.7 %copy-start.12 = (f32[64]{0:T(128)S(1)}, f32[64]{0:T(128)}, u32[]{:S(2)}) copy-start(f32[64]{0:T(128)} %param.28) | copy-start | bytes 772
  4.8 27.7 %copy-start.13 = (f32[64]{0:T(128)S(1)}, f32[64]{0:T(128)}, u32[]{:S(2)}) copy-start(f32[64]{0:T(128)} %param.27) | copy-start | bytes 772
  4.9 27.7 %copy-start.14 = (f32[64]{0:T(128)S(1)}, f32[64]{0:T(128)}, u32[]{:S(2)}) copy-start(f32[64]{0:T(128)} %param.26) | copy-start | bytes 772
  4.9 36.3 %copy-start.5 = (bf16[20,3,1024]{2,0,1:T(8,128)(2,1)S(1)}, bf16[20,3,1024]{2,0,1:T(8,128)(2,1)}, u32[]{:S(2)}) copy-start(bf16[20,3,1024]{2,0,1:T(8,128)(2,1)} %param.25) | copy-start | bytes 368644
  4.9 36.3 %copy-start.6 = (bf16[4,1024]{1,0:T(4,128)(2,1)S(1)}, bf16[4,1024]{1,0:T(4,128)(2,1)}, u32[]{:S(2)}) copy-start(bf16[4,1024]{1,0:T(4,128)(2,1)} %refs_5_.1) | copy-start | bytes 24580
  6.5 26.1 %collective-permute-start.3 = (bf16[48,1152]{1,0:T(8,128)(2,1)S(1)}, bf16[48,1152]{1,0:T(8,128)(2,1)S(1)}, u32[]{:S(2)}, u32[]{:S(2)}) collective-permute-start(bf16[48,1152]{1,0:T(8,128)(2,1)S(1)} %get-tuple-element.26.refs_0_), channel_id=1, source_target_pairs={{0,1},{1,0},{2,3},{3,2},{4,5},{5,4},{6,7},{7,6},{8,9},{9,8},{10,11... | collective-permute-start | bytes 331784 | tf_op jit(solution)/shard_map/ppermute | solution.py:27
  7.1 25.9 %collective-permute-start.4 = (bf16[48,1152]{1,0:T(8,128)(2,1)S(1)}, bf16[48,1152]{1,0:T(8,128)(2,1)S(1)}, u32[]{:S(2)}, u32[]{:S(2)}) collective-permute-start(bf16[48,1152]{1,0:T(8,128)(2,1)S(1)} %get-tuple-element.26.refs_0_), channel_id=1, source_target_pairs={{0,2},{1,3},{2,0},{3,1},{4,6},{5,7},{6,4},{7,5},{8,10},{9,11},{10,... | collective-permute-start | bytes 331784 | tf_op jit(solution)/shard_map/ppermute | solution.py:27
  27.8 25.1 %collective-permute-start = (bf16[96,1024]{1,0:T(8,128)(2,1)S(1)}, bf16[96,1024]{1,0:T(8,128)(2,1)S(1)}, u32[]{:S(2)}, u32[]{:S(2)}) collective-permute-start(bf16[96,1024]{1,0:T(8,128)(2,1)S(1)} %get-tuple-element.23), channel_id=1, source_target_pairs={{0,1},{1,0},{2,3},{3,2},{4,5},{5,4},{6,7},{7,6},{8,9},{9,8},{10,11... | collective-permute-start | bytes 589832 | tf_op jit(solution)/shard_map/ppermute | solution.py:27
  28.0 24.9 %collective-permute-start.1 = (bf16[96,1024]{1,0:T(8,128)(2,1)S(1)}, bf16[96,1024]{1,0:T(8,128)(2,1)S(1)}, u32[]{:S(2)}, u32[]{:S(2)}) collective-permute-start(bf16[96,1024]{1,0:T(8,128)(2,1)S(1)} %get-tuple-element.24), channel_id=1, source_target_pairs={{0,2},{1,3},{2,0},{3,1},{4,6},{5,7},{6,4},{7,5},{8,10},{9,11},{10,... | collective-permute-start | bytes 589832 | tf_op jit(solution)/shard_map/ppermute | solution.py:27
  28.3 24.6 %collective-permute-start.2 = (bf16[96,1024]{1,0:T(8,128)(2,1)S(1)}, bf16[96,1024]{1,0:T(8,128)(2,1)S(1)}, u32[]{:S(2)}, u32[]{:S(2)}) collective-permute-start(bf16[96,1024]{1,0:T(8,128)(2,1)S(1)} %get-tuple-element.25), channel_id=1, source_target_pairs={{0,3},{1,2},{2,1},{3,0},{4,7},{5,6},{6,5},{7,4},{8,11},{9,10},{10,... | collective-permute-start | bytes 589832 | tf_op jit(solution)/shard_map/ppermute | solution.py:27
  32.6 8.6 %collective-permute-start.5 = (bf16[48,1152]{1,0:T(8,128)(2,1)S(1)}, bf16[48,1152]{1,0:T(8,128)(2,1)S(1)}, u32[]{:S(2)}, u32[]{:S(2)}) collective-permute-start(bf16[48,1152]{1,0:T(8,128)(2,1)S(1)} %get-tuple-element.26.refs_0_), channel_id=1, source_target_pairs={{0,3},{1,2},{2,1},{3,0},{4,7},{5,6},{6,5},{7,4},{8,11},{9,10},{10,... | collective-permute-start | bytes 331784 | tf_op jit(solution)/shard_map/ppermute | solution.py:27
  42.0 7.0 %copy-start = (f32[20,64,16,256]{3,2,1,0:T(8,128)S(1)}, f32[20,64,16,256]{3,2,1,0:T(8,128)}, u32[]{:S(2)}) copy-start(f32[20,64,16,256]{3,2,1,0:T(8,128)} %param.31) | copy-start | bytes 62914564
  48.9 34.0 %slice-start = ((bf16[20,3,64,16]{2,3,1,0:T(8,128)(2,1)}), bf16[20,1,64,16]{2,3,1,0:T(8,128)(2,1)S(1)}, s32[]{:S(2)}) async-start(bf16[20,3,64,16]{2,3,1,0:T(8,128)(2,1)} %param.24), calls=%async_computation | async-start | bytes 163840 | tf_op jit(solution)/shard_map/slice | solution.py:537
  53.6 13.5 %collective-permute-start.6 = (bf16[48,1152]{1,0:T(8,128)(2,1)S(1)}, bf16[48,1152]{1,0:T(8,128)(2,1)S(1)}, u32[]{:S(2)}, u32[]{:S(2)}) collective-permute-start(bf16[48,1152]{1,0:T(8,128)(2,1)S(1)} %get-tuple-element.29.refs_0_), channel_id=1, source_target_pairs={{0,4},{4,0},{8,12},{12,8},{1,5},{5,1},{9,13},{13,9},{2,6},{6,2},{1... | collective-permute-start | bytes 331784 | tf_op jit(solution)/shard_map/ppermute | solution.py:27
  55.3 11.6 %collective-permute-start.7 = (bf16[48,1152]{1,0:T(8,128)(2,1)S(1)}, bf16[48,1152]{1,0:T(8,128)(2,1)S(1)}, u32[]{:S(2)}, u32[]{:S(2)}) collective-permute-start(bf16[48,1152]{1,0:T(8,128)(2,1)S(1)} %get-tuple-element.29.refs_0_), channel_id=1, source_target_pairs={{0,8},{4,12},{8,0},{12,4},{1,9},{5,13},{9,1},{13,5},{2,10},{6,14},... | collective-permute-start | bytes 331784 | tf_op jit(solution)/shard_map/ppermute | solution.py:27
  57.9 8.0 %collective-permute-start.8 = (bf16[48,1152]{1,0:T(8,128)(2,1)S(1)}, bf16[48,1152]{1,0:T(8,128)(2,1)S(1)}, u32[]{:S(2)}, u32[]{:S(2)}) collective-permute-start(bf16[48,1152]{1,0:T(8,128)(2,1)S(1)} %get-tuple-element.29.refs_0_), channel_id=1, source_target_pairs={{0,12},{4,8},{8,4},{12,0},{1,13},{5,9},{9,5},{13,1},{2,14},{6,10},... | collective-permute-start | bytes 331784 | tf_op jit(solution)/shard_map/ppermute | solution.py:27
  67.4 3.2 %collective-permute-start.9 = (f32[48,128]{1,0:T(8,128)S(1)}, f32[48,128]{1,0:T(8,128)S(1)}, u32[]{:S(2)}, u32[]{:S(2)}) collective-permute-start(f32[48,128]{1,0:T(8,128)S(1)} %select_add_fusion.refs_4_), channel_id=1, source_target_pairs={{0,1},{1,0},{2,3},{3,2},{4,5},{5,4},{6,7},{7,6},{8,9},{9,8},{10,11... | collective-permute-start | bytes 73736 | tf_op jit(solution)/shard_map/ppermute | solution.py:27
  67.5 4.1 %collective-permute-start.10 = (f32[48,128]{1,0:T(8,128)S(1)}, f32[48,128]{1,0:T(8,128)S(1)}, u32[]{:S(2)}, u32[]{:S(2)}) collective-permute-start(f32[48,128]{1,0:T(8,128)S(1)} %select_add_fusion.refs_4_), channel_id=1, source_target_pairs={{0,2},{1,3},{2,0},{3,1},{4,6},{5,7},{6,4},{7,5},{8,10},{9,11},{10,... | collective-permute-start | bytes 73736 | tf_op jit(solution)/shard_map/ppermute | solution.py:27
  68.1 3.5 %collective-permute-start.11 = (f32[48,128]{1,0:T(8,128)S(1)}, f32[48,128]{1,0:T(8,128)S(1)}, u32[]{:S(2)}, u32[]{:S(2)}) collective-permute-start(f32[48,128]{1,0:T(8,128)S(1)} %select_add_fusion.refs_4_), channel_id=1, source_target_pairs={{0,3},{1,2},{2,1},{3,0},{4,7},{5,6},{6,5},{7,4},{8,11},{9,10},{10,... | collective-permute-start | bytes 73736 | tf_op jit(solution)/shard_map/ppermute | solution.py:27
  71.6 5.8 %copy-start.2 = (bf16[256,16,2048]{2,1,0:T(8,128)(2,1)S(1)}, bf16[256,16,2048]{2,1,0:T(8,128)(2,1)}, u32[]{:S(2)}) copy-start(bf16[256,16,2048]{2,1,0:T(8,128)(2,1)} %param.30) | copy-start | bytes 50331652
  81.0 22.4 %collective-permute-start.14 = (bf16[48,512]{1,0:T(8,128)(2,1)S(1)}, bf16[48,512]{1,0:T(8,128)(2,1)S(1)}, u32[]{:S(2)}, u32[]{:S(2)}) collective-permute-start(bf16[48,512]{1,0:T(8,128)(2,1)S(1)} %get-tuple-element.33), channel_id=1, source_target_pairs={{0,3},{1,2},{2,1},{3,0},{4,7},{5,6},{6,5},{7,4},{8,11},{9,10},{10,... | collective-permute-start | bytes 147464 | tf_op jit(solution)/shard_map/ppermute | solution.py:27
  82.1 21.3 %collective-permute-start.13 = (bf16[48,512]{1,0:T(8,128)(2,1)S(1)}, bf16[48,512]{1,0:T(8,128)(2,1)S(1)}, u32[]{:S(2)}, u32[]{:S(2)}) collective-permute-start(bf16[48,512]{1,0:T(8,128)(2,1)S(1)} %get-tuple-element.32), channel_id=1, source_target_pairs={{0,2},{1,3},{2,0},{3,1},{4,6},{5,7},{6,4},{7,5},{8,10},{9,11},{10,... | collective-permute-start | bytes 147464 | tf_op jit(solution)/shard_map/ppermute | solution.py:27
  82.8 20.6 %collective-permute-start.12 = (bf16[48,512]{1,0:T(8,128)(2,1)S(1)}, bf16[48,512]{1,0:T(8,128)(2,1)S(1)}, u32[]{:S(2)}, u32[]{:S(2)}) collective-permute-start(bf16[48,512]{1,0:T(8,128)(2,1)S(1)} %get-tuple-element.31), channel_id=1, source_target_pairs={{0,1},{1,0},{2,3},{3,2},{4,5},{5,4},{6,7},{7,6},{8,9},{9,8},{10,11... | collective-permute-start | bytes 147464 | tf_op jit(solution)/shard_map/ppermute | solution.py:27
  83.7 7.0 %copy-start.1 = (f32[20,64,16,256]{3,2,1,0:T(8,128)S(1)}, f32[20,64,16,256]{3,2,1,0:T(8,128)}, u32[]{:S(2)}) copy-start(f32[20,64,16,256]{3,2,1,0:T(8,128)} %param.31) | copy-start | bytes 62914564

commit v2 on v1

v2 whole, which is shorter than its diff:
```python
import functools

import jax
import jax.numpy as jnp
from jax import lax
from jax.experimental import pallas as pl
from jax.experimental.pallas import tpu as pltpu
from jax.sharding import PartitionSpec as P

HEADS = 256
HEAD_DIM = 64
STATE = 256
NGROUPS = 8
LANES = 128
MIB = 2**20
PROJ_MIB = 56
NEXT_PROJ_MIB = 20
READ_MIB = 8
WRITE_MIB = 8
OUT_MIB = 36

EPSILON = 1e-05

F32 = jnp.float32
BF16 = jnp.bfloat16
VMEM_SPEC = pl.BlockSpec(memory_space=pltpu.VMEM)
SMEM_SPEC = pl.BlockSpec(memory_space=pltpu.SMEM)
ANY_SPEC = pl.BlockSpec(memory_space=pl.ANY)
HBM_SPEC = pl.BlockSpec(memory_space=pltpu.HBM)


def exchanged(value, axis, mask):
    return lax.ppermute(value, axis, [(i, i ^ mask) for i in range(lax.axis_size(axis))])


def from_all(value, axis):
    return [value] + [exchanged(value, axis, mask) for mask in range(1, lax.axis_size(axis))]


def silu(value):
    return value / (1.0 + jnp.exp(-value))


def iota(shape, dim):
    return lax.broadcasted_iota(jnp.int32, shape, dim)


def params(mib, **more):
    return pltpu.CompilerParams(vmem_limit_bytes=mib * MIB, **more)


def cost(flops, nbytes):
    return pl.CostEstimate(flops=int(flops), bytes_accessed=int(nbytes), transcendentals=0)


def spread_heads(heads, chan):
    shape = (heads, heads * chan)
    return (iota(shape, 1) // chan == iota(shape, 0)).astype(F32).astype(BF16)


def channel_lanes(refs, half, shape):
    history, taps, offset, gain = refs
    seqs, kept, chan, heads = history.shape
    values = [ref[...].reshape(-1, heads) for ref in (history, taps, offset, gain)]
    values = jnp.concatenate([value.astype(F32) for value in values], axis=0).astype(BF16)
    count = values.shape[0]
    wide = jnp.dot(values, spread_heads(heads, chan), preferred_element_type=F32)
    keep = iota(wide.shape, 0) % chan == iota(wide.shape, 1) % chan
    wide = jnp.where(keep, wide, 0.0).astype(BF16)
    given = iota((shape[0], count), 1) // chan
    target = jnp.where(given < seqs * kept, given % kept * half + given // kept, given - seqs * kept + kept * half)
    collect = (target == iota((shape[0], count), 0)).astype(F32).astype(BF16)
    return jnp.dot(collect, wide, preferred_element_type=F32).astype(BF16)


def kept_channels_kernel(history_ref, fresh_ref, out_ref):
    seqs, kept, chan, heads = history_ref.shape
    half = fresh_ref.shape[0] // 2
    shape = (2 * seqs * chan, 2 * half)
    wanted = iota(shape, 0) // chan
    wanted = wanted // seqs * half + wanted % seqs
    repeat = (wanted == iota(shape, 1)).astype(F32).astype(BF16)
    wide = jnp.dot(repeat, fresh_ref[...], preferred_element_type=F32)
    keep = iota(wide.shape, 0) % chan == iota(wide.shape, 1) % chan
    wide = jnp.where(keep, wide, 0.0).astype(BF16)
    shape = (heads * chan, heads)
    collect = (iota(shape, 0) // chan == iota(shape, 1)).astype(F32).astype(BF16)
    out = jnp.dot(wide, collect, preferred_element_type=F32)
    for seq in range(seqs):
        out_ref[seq, 0] = history_ref[seq, kept - 1]
        for token in range(2):
            row = (token * seqs + seq) * chan
            out_ref[seq, kept - 2 + token] = out[row : row + chan].astype(BF16)


def kept_channels(history, fresh):
    return pl.pallas_call(
        kept_channels_kernel,
        out_shape=jax.ShapeDtypeStruct(history.shape, BF16),
        in_specs=[VMEM_SPEC, VMEM_SPEC],
        out_specs=VMEM_SPEC,
        compiler_params=params(10),
        cost_estimate=cost(100 * fresh.size, 4 * fresh.size),
        name="kept_channels",
    )(history, fresh)


def proj_kernel(*refs, slots, first, narrow, chan, half, small):
    me_ref, w_ref = refs[:2]
    if small:
        x_ref, bc_ref, dt_ref, spread, mover = refs[2:7]
        x_held, bc_held, dt_held, x_sem, bc_sem, dt_sem = refs[-6:]
        refs = refs[7:-6]
    else:
        spread, mover = refs[2:4]
        channel_refs = refs[4:8]
        later_ref, later, lanes_ref = refs[8:11]
        later_sem = refs[-1]
        refs = refs[11:-1]
    outs = refs[:narrow]
    held, flat, total, chunks, held_sem, flat_sem = refs[narrow:]
    feats = w_ref.shape[0]
    rows = spread.shape[0] // 2
    span = mover.shape[0]
    pair = held.shape[1]
    blocks = total.shape[1] // LANES
    steps = blocks // pair

    def copies(i):
        return [
            pltpu.make_async_copy(
                w_ref.at[:, first + i * pair + j], held.at[i % slots, j], held_sem.at[i % slots, j]
            )
            for j in range(pair)
        ]

    def flat_copy(i):
        source = held.at[i % slots].reshape(pair * 2 * feats, LANES)
        return pltpu.make_async_copy(source, flat.at[i % 2], flat_sem.at[i % 2])

    parts = 0 if small else later.shape[0]

    def later_copy(i):
        return pltpu.make_async_copy(later_ref.at[i], later.at[i], later_sem.at[i])

    if small:
        x_copy = pltpu.make_async_copy(x_ref, x_held, x_sem)
        bc_copy = pltpu.make_async_copy(bc_ref, bc_held, bc_sem)
        dt_copy = pltpu.make_async_copy(dt_ref, dt_held, dt_sem)
        x_copy.start()
    for i in range(min(slots, steps)):
        for copy in copies(i):
            copy.start()
    if small:
        bc_copy.start()
        dt_copy.start()

    if small:
        x_copy.wait()
        seqs, tokens, _ = x_held.shape
        given = iota((rows, tokens * seqs), 1)
        wanted = iota((rows, tokens * seqs), 0)
        order = (given % tokens * half + given // tokens == wanted).astype(F32).astype(BF16)
        x = jnp.dot(order, x_held[...].reshape(tokens * seqs, feats), preferred_element_type=F32)
        x = x.astype(BF16)
        piece = min(256, feats)
        pieces = feats // piece
        stacked = jnp.concatenate([x[:, i * piece : (i + 1) * piece] for i in range(pieces)], axis=0)
        place = iota((piece, 2 * piece), 1) - 2 * iota((piece, 2 * piece), 0)
        for z in range(2):
            one_hot = (place == z).astype(F32).astype(BF16)
            moved = jnp.dot(stacked, one_hot, preferred_element_type=F32).astype(BF16)
            for i in range(pieces):
                columns = slice(2 * i * piece, 2 * (i + 1) * piece)
                spread[z * rows : (z + 1) * rows, columns] = moved[i * rows : (i + 1) * rows]
        column = iota((span, span), 0)
        target = (column % HEAD_DIM) // chan * (span // narrow) + column // HEAD_DIM * chan + column % chan
        mover[...] = (target == iota((span, span), 1)).astype(F32).astype(BF16)

    else:
        lanes_ref[...] = channel_lanes(channel_refs, half, lanes_ref.shape)

    def arrived(i):
        for copy in copies(i):
            copy.wait()
        flat_copy(i).start()

    arrived(0)
    for i in range(steps):
        flat_copy(i).wait()
        if i + slots < steps:
            for copy in copies(i + slots):
                copy.start()
        for j in range(i * parts // steps, (i + 1) * parts // steps):
            later_copy(j).start()
        if i + 1 < steps:
            arrived(i + 1)
        weight = jnp.concatenate([flat[i % 2, j * 2 * feats : (j + 1) * 2 * feats] for j in range(pair)], axis=1)
        columns = slice(i * pair * LANES, (i + 1) * pair * LANES)
        total[:, columns] = jnp.dot(spread[...], weight, preferred_element_type=F32).astype(BF16)
        if (i + 1) * pair * LANES % span == 0:
            q = (i + 1) * pair * LANES // span - 1
            part = span // narrow
            moved = jnp.dot(total[:, q * span : (q + 1) * span], mover[...], preferred_element_type=F32)
            for n in range(narrow):
                chunks[n, :, q * part : (q + 1) * part] = moved[:, n * part : (n + 1) * part].astype(BF16)
    if small:
        bc_copy.wait()
        dt_copy.wait()
        bc_part = jnp.dot(x, bc_held[...], preferred_element_type=F32)
        dt_part = lax.dot_general(x, dt_held[...], (((1,), (1,)), ((), ())), preferred_element_type=F32)
        chunk_cols, cols = chunks.shape[2], outs[0].shape[1]
        pad = jnp.zeros((rows, 2 * (cols - chunk_cols) - bc_part.shape[1] - dt_part.shape[1]), F32)
        sums = jnp.concatenate([bc_part, dt_part, pad], axis=1).astype(BF16)
        for mask in range(narrow):
            outs[mask][:rows, chunk_cols:] = sums[:, : cols - chunk_cols]
            outs[mask][rows:, chunk_cols:] = sums[:, cols - chunk_cols :]
    for mask in range(narrow):
        outs[mask][:, : chunks.shape[2]] = chunks[me_ref[1] ^ mask]
    for j in range(parts):
        later_copy(j).wait()


def proj(me, weight, given, half, narrow, chan, first, blocks, small, slots=4):
    feats, _, cols = weight.shape
    rows = 2 * half
    pair = 2 if blocks % 2 == 0 else 1
    by_block = weight.reshape(feats, 2, cols // LANES, LANES).transpose(0, 2, 1, 3)
    cols = blocks * LANES // narrow
    scratch = [
        pltpu.VMEM((slots, pair, feats, 2, LANES), BF16),
        pltpu.VMEM((2, pair * 2 * feats, LANES), BF16),
        pltpu.VMEM((2 * rows, blocks * LANES), BF16),
        pltpu.VMEM((narrow, 2 * rows, blocks * LANES // narrow), BF16),
        pltpu.SemaphoreType.DMA((slots, pair)),
        pltpu.SemaphoreType.DMA((2,)),
    ]
    specs = [VMEM_SPEC] * len(given)
    nbytes = 4 * feats * blocks * LANES
    if small:
        inputs, bc_weight, dt_weight_t = given
        span = min(narrow, blocks) * LANES
        out_shape = [
            jax.ShapeDtypeStruct((2 * rows, 2 * feats), BF16),
            jax.ShapeDtypeStruct((span, span), BF16),
        ]
        cols += -(-(bc_weight.shape[1] + dt_weight_t.shape[0]) // (2 * LANES)) * LANES
        scratch += [pltpu.VMEM(value.shape, BF16) for value in given] + [pltpu.SemaphoreType.DMA] * 3
        specs = [HBM_SPEC] * 3
        nbytes += 2 * (bc_weight.size + dt_weight_t.size)
    else:
        history, later = given[2], given[-1]
        specs[-1] = HBM_SPEC
        nbytes += later.size * later.dtype.itemsize
        scratch += [pltpu.SemaphoreType.DMA((later.shape[0],))]
        out_shape = [jax.ShapeDtypeStruct(later.shape, later.dtype)]
        out_shape += [jax.ShapeDtypeStruct((3 * half + 8, history.shape[2] * history.shape[3]), BF16)]
    out_shape += [jax.ShapeDtypeStruct((2 * rows, cols), BF16)] * narrow
    return pl.pallas_call(
        functools.partial(
            proj_kernel, slots=slots, first=first, narrow=narrow, chan=chan, half=half, small=small
        ),
        out_shape=out_shape,
        in_specs=[SMEM_SPEC, HBM_SPEC] + specs,
        out_specs=[VMEM_SPEC] * len(out_shape),
        scratch_shapes=scratch,
        compiler_params=params(PROJ_MIB if small else NEXT_PROJ_MIB),
        cost_estimate=cost(rows * nbytes, nbytes),
        name="proj_small" if small else "proj",
    )(me, by_block, *given)


def conv_pair(history, fresh, taps, offset):
    window = list(history) + list(fresh)
    outputs = []
    for token in range(2):
        summed = offset
        for tap in range(4):
            summed = summed + taps[tap : tap + 1] * window[token + tap]
        outputs.append(silu(summed))
    return outputs


def summed_refs(refs):
    total = refs[0][...].astype(F32)
    for ref in refs[1:]:
        total = total + ref[...].astype(F32)
    return total


def bc_conv_kernel(*refs, parts, seqs):
    history_ref, taps_ref, offset_ref, conv_ref, kept_ref, dt_ref, chan_ref = refs[parts:]
    rows, chunk_cols = conv_ref.shape[0], chan_ref.shape[1]
    both = summed_refs(refs[:parts])
    chan_ref[...] = both[:, :chunk_cols].astype(BF16)
    summed = jnp.concatenate([both[:rows, chunk_cols:], both[rows:, chunk_cols:]], axis=1)
    half = summed.shape[0] // 2
    cols = taps_ref.shape[1]
    proj = summed.astype(BF16).astype(F32)
    dt_ref[...] = proj[:, cols : cols + LANES]
    fresh = [proj[:seqs, :cols], proj[half : half + seqs, :cols]]
    history = [history_ref[i].astype(F32) for i in range(3)]
    conv_ref[...] = jnp.zeros_like(conv_ref)
    for token, value in enumerate(conv_pair(history, fresh, taps_ref[...].astype(F32), offset_ref[...].astype(F32))):
        conv_ref[token * half : token * half + seqs] = value
    kept_ref[0] = history_ref[2]
    kept_ref[1] = fresh[0].astype(BF16)
    kept_ref[2] = fresh[1].astype(BF16)


def bc_conv(parts, history, taps, offset, chunk_cols):
    rows = parts[0].shape[0]
    cols = taps.shape[1]
    return pl.pallas_call(
        functools.partial(bc_conv_kernel, parts=len(parts), seqs=history.shape[1]),
        out_shape=(
            jax.ShapeDtypeStruct((rows // 2, cols), F32),
            jax.ShapeDtypeStruct(history.shape, BF16),
            jax.ShapeDtypeStruct((rows // 2, LANES), F32),
            jax.ShapeDtypeStruct((rows, chunk_cols), BF16),
        ),
        in_specs=[VMEM_SPEC] * (len(parts) + 3),
        out_specs=(VMEM_SPEC,) * 4,
        compiler_params=params(8),
        cost_estimate=cost(30 * rows * cols, 8 * rows * cols),
        name="bc_conv",
    )(*parts, history, taps, offset)


def state_read_kernel(bc_ref, state_ref, read_ref, *, groups):
    seqs, rows, _ = state_ref.shape
    half = bc_ref.shape[0] // 2
    span = rows // groups
    read_ref[...] = jnp.zeros_like(read_ref)
    for seq in range(seqs):
        for g in range(groups):
            cols = slice((2 * g + 1) * STATE, (2 * g + 2) * STATE)
            both = jnp.concatenate([bc_ref[t * half + seq : t * half + seq + 1, cols] for t in range(2)], axis=0)
            held = state_ref[seq, g * span : (g + 1) * span].astype(BF16)
            out = lax.dot_general(both.astype(BF16), held, (((1,), (1,)), ((), ())), preferred_element_type=F32)
            for t in range(2):
                read_ref[t * half + seq : t * half + seq + 1, g * span : (g + 1) * span] = out[t : t + 1]


def state_read(bc, state, groups):
    seqs, rows, _ = state.shape
    return pl.pallas_call(
        functools.partial(state_read_kernel, groups=groups),
        out_shape=jax.ShapeDtypeStruct((bc.shape[0], rows), F32),
        in_specs=[VMEM_SPEC, VMEM_SPEC],
        out_specs=VMEM_SPEC,
        compiler_params=params(READ_MIB),
        cost_estimate=cost(4 * state.size, 4 * state.size),
        name="state_read",
    )(bc, state)


def readout_kernel(*refs, parts, groups, heads, chan):
    done_ref, part_refs = refs[0], refs[1 : parts + 1]
    lanes_ref, read_ref, bc_ref, dt_ref, heads_ref = refs[parts + 1 : parts + 6]
    sent_ref, fresh_ref, scale_ref, decay_ref = refs[parts + 6 :]
    columns = [done_ref[...].astype(F32)]
    if part_refs:
        columns.append(summed_refs(part_refs).astype(BF16).astype(F32))
    proj = jnp.concatenate(columns, axis=1)
    half = proj.shape[0] // 4
    width = proj.shape[1]
    gates = [proj[:half], proj[half : 2 * half]]
    fresh = [proj[2 * half : 3 * half], proj[3 * half :]]
    fresh_ref[...] = proj[2 * half :].astype(BF16)
    lanes = lanes_ref[...].astype(F32)
    history = [lanes[i * half : (i + 1) * half] for i in range(3)]
    taps, offset, gain = (lanes[3 * half + i : 3 * half + j] for i, j in ((0, 4), (4, 5), (5, 6)))
    x = conv_pair(history, fresh, taps, offset)

    bias, rate, skip = heads_ref[0:1], jnp.exp(heads_ref[1:2]), heads_ref[2:3]
    raw = dt_ref[:, :heads] + bias
    step = jnp.maximum(raw, 0.0) + jnp.log1p(jnp.exp(-jnp.abs(raw)))
    decay = jnp.exp(-step * rate)
    decay_ref[...] = decay[:half] * decay[half:]
    repeat = (iota((heads, width), 1) // chan == iota((heads, width), 0)).astype(F32)
    packed = jnp.concatenate([step, decay, jnp.broadcast_to(skip, (8, heads))], axis=0)
    spread = jnp.dot(packed, repeat, preferred_element_type=F32, precision=lax.Precision.HIGHEST)
    steps = [spread[:half], spread[half : 2 * half]]
    decays = [spread[2 * half : 3 * half], spread[3 * half : 4 * half]]
    skips = spread[4 * half : 4 * half + 1]

    span = width // groups

    def dots(b_token, c_token):
        out = []
        for g in range(groups):
            b = bc_ref[b_token * half : (b_token + 1) * half, 2 * g * STATE : (2 * g + 1) * STATE]
            c = bc_ref[c_token * half : (c_token + 1) * half, (2 * g + 1) * STATE : (2 * g + 2) * STATE]
            out.append(jnp.broadcast_to(jnp.sum(b * c, axis=1, keepdims=True), (half, span)))
        return jnp.concatenate(out, axis=1)

    first = steps[0] * x[0]
    second = steps[1] * x[1]
    carried = decays[1] * first
    y = [
        decays[0] * read_ref[:half] + first * dots(0, 0) + skips * x[0],
        decays[0] * decays[1] * read_ref[half:] + carried * dots(0, 1) + second * dots(1, 1) + skips * x[1],
    ]
    scale_ref[:half] = carried
    scale_ref[half:] = second
    lane = iota((half, LANES), 1)
    for token in range(2):
        gated = y[token] * silu(gates[token])
        rows = slice(token * half, (token + 1) * half)
        sent_ref[rows, :width] = (gated * gain).astype(BF16)
        squares = jnp.zeros((half, LANES), F32)
        for g in range(groups):
            part = gated[:, g * span : (g + 1) * span]
            total = jnp.sum(part * part, axis=1, keepdims=True)
            high = total.astype(BF16).astype(F32)
            squares = squares + jnp.where(lane == 2 * g, high, 0.0) + jnp.where(lane == 2 * g + 1, total - high, 0.0)
        sent_ref[rows, width:] = squares.astype(BF16)


def readout(done, parts, lanes, read, bc, dt, head_vals, groups, chan):
    rows, width = read.shape
    heads = head_vals.shape[1]
    return pl.pallas_call(
        functools.partial(readout_kernel, parts=len(parts), groups=groups, heads=heads, chan=chan),
        out_shape=(
            jax.ShapeDtypeStruct((rows, width + LANES), BF16),
            jax.ShapeDtypeStruct((rows, width), BF16),
            jax.ShapeDtypeStruct((rows, width), F32),
            jax.ShapeDtypeStruct((rows // 2, heads), F32),
        ),
        in_specs=[VMEM_SPEC] * (len(parts) + 6),
        out_specs=(VMEM_SPEC,) * 4,
        compiler_params=params(16),
        cost_estimate=cost(100 * rows * width, 12 * rows * width),
        name="readout",
    )(done, *parts, lanes, read, bc, dt, head_vals)


def state_write_kernel(*refs, groups, heads, first, count, prepare):
    if prepare:
        scale_ref, decay_ref, bc_ref, state_ref, new_ref, left, decays = refs[:7]
        refs = refs[7:]
    else:
        left, decays, bc_ref, state_ref, _, _, new_ref, mark_ref = refs[:8]
        refs = refs[8:]
        mark_ref[...] = jnp.zeros_like(mark_ref)
    right, made, sems = refs
    seqs, rows, _ = state_ref.shape
    half = bc_ref.shape[0] // 2
    span = rows // groups
    chan = rows // heads
    slots = made.shape[0]
    right[...] = jnp.zeros_like(right)
    if prepare:
        scale = scale_ref[...]
        high = scale.astype(BF16).astype(F32)
        pad = jnp.zeros((left.shape[1] - 6 * half, rows), F32)
        left[...] = jnp.concatenate([high, scale - high, high, pad], axis=0).T.astype(BF16)
        by_head = decay_ref[...].T
        for s in range(seqs):
            decays[s * heads : (s + 1) * heads] = jnp.broadcast_to(by_head[:, s : s + 1], (heads, LANES))

    def out_copy(seq):
        slot = (seq - first) % slots
        return pltpu.make_async_copy(made.at[slot], new_ref.at[seq], sems.at[slot])

    for seq in range(first, first + count):
        slot = (seq - first) % slots
        side = (seq - first) % right.shape[0]
        values = []
        for t in range(2):
            row = bc_ref[t * half + seq : t * half + seq + 1, :]
            values.append(jnp.concatenate([row[:, 2 * g * STATE : (2 * g + 1) * STATE] for g in range(groups)], axis=1))
        high = [value.astype(BF16).astype(F32) for value in values]
        low = [value - top for value, top in zip(values, high)]
        for block, value in enumerate(high + high + low):
            right[side, block * half + seq : block * half + seq + 1, :] = value
        if seq - first >= slots:
            out_copy(seq - slots).wait()
        for g in range(groups):
            here = slice(g * span, (g + 1) * span)
            factor = right[side, :, g * STATE : (g + 1) * STATE].astype(BF16)
            added = jnp.dot(left[here], factor, preferred_element_type=F32)
            for h in range(span // chan):
                head = g * (span // chan) + h
                decay = decays[seq * heads + head : seq * heads + head + 1, :]
                decay = jnp.concatenate([decay] * (STATE // LANES), axis=1)
                made[slot, head * chan : (head + 1) * chan] = (
                    decay * state_ref[seq, head * chan : (head + 1) * chan] + added[h * chan : (h + 1) * chan]
                )
        out_copy(seq).start()
        for block in range(6):
            right[side, block * half + seq : block * half + seq + 1, :] = jnp.zeros((1, right.shape[2]), F32)
    for seq in range(max(first, first + count - slots), first + count):
        out_copy(seq).wait()


def state_write(given, bc, state, groups, heads, first, count, before=None, after=None):
    seqs, rows, _ = state.shape
    half = bc.shape[0] // 2
    prepare = before is None
    depth = -(-6 * half // LANES) * LANES
    scratch = [
        pltpu.VMEM((2, depth, groups * STATE), F32),
        pltpu.VMEM((3, rows, STATE), F32),
        pltpu.SemaphoreType.DMA((3,)),
    ]
    if prepare:
        more = [
            jax.ShapeDtypeStruct((rows, depth), BF16),
            jax.ShapeDtypeStruct((seqs * heads, LANES), F32),
        ]
        extra = []
    else:
        more = [jax.ShapeDtypeStruct((8, LANES), F32)]
        extra = [before, after]
    nbytes = 4 * count * rows * STATE
    return pl.pallas_call(
        functools.partial(
            state_write_kernel, groups=groups, heads=heads, first=first, count=count, prepare=prepare
        ),
        out_shape=[jax.ShapeDtypeStruct(state.shape, F32)] + more,
        in_specs=[VMEM_SPEC] * 4 + [HBM_SPEC] * len(extra),
        out_specs=[HBM_SPEC] + [VMEM_SPEC] * len(more),
        scratch_shapes=scratch,
        input_output_aliases={} if prepare else {4: 0},
        compiler_params=params(WRITE_MIB),
        cost_estimate=cost(nbytes, 2 * nbytes),
        name="state_write",
    )(*given, bc, state, *extra)


def squares_kernel(me_ref, *refs, wide, groups):
    sent, out_ref = refs[:wide], refs[-1]
    rows, lanes = out_ref.shape
    lane = iota((rows, lanes), 1)
    total = jnp.zeros((rows, lanes), F32)
    for mask in range(wide):
        owner = me_ref[0] ^ mask
        value = sent[mask][:, sent[mask].shape[1] - lanes :].astype(F32)
        for g in range(groups):
            own = value[:, 2 * g : 2 * g + 1] + value[:, 2 * g + 1 : 2 * g + 2]
            total = total + jnp.where(lane == owner * groups + g, own, 0.0)
    out_ref[...] = total


def all_squares(me, sent, groups, after):
    wide = len(sent)
    return pl.pallas_call(
        functools.partial(squares_kernel, wide=wide, groups=groups),
        out_shape=jax.ShapeDtypeStruct((sent[0].shape[0], LANES), F32),
        in_specs=[SMEM_SPEC] + [VMEM_SPEC] * wide + [ANY_SPEC],
        out_specs=VMEM_SPEC,
        compiler_params=params(8),
        cost_estimate=cost(LANES * LANES * wide, 4 * LANES * LANES * wide),
        name="all_squares",
    )(me, *sent, after)


def out_proj_kernel(me_ref, *refs, wide, groups):
    sent = refs[:wide]
    w_ref, _, made_ref, held, sems = refs[wide:]
    width = w_ref.shape[0] // wide
    span = width // groups

    def copy(mask):
        owner = me_ref[0] ^ mask
        rows = pl.ds(pl.multiple_of(owner * width, width), width)
        return pltpu.make_async_copy(w_ref.at[rows], held.at[mask], sems.at[mask])

    for mask in range(wide):
        copy(mask).start()
    for mask in range(wide):
        copy(mask).wait()
        for g in range(groups):
            rows = slice(g * span, (g + 1) * span)
            product = jnp.dot(sent[mask][:, rows], held[mask, rows], preferred_element_type=F32)
            made_ref[mask * groups + g] = product


def out_proj(me, sent, weight, groups, after):
    wide = len(sent)
    rows = sent[0].shape[0]
    depth, cols = weight.shape
    return pl.pallas_call(
        functools.partial(out_proj_kernel, wide=wide, groups=groups),
        out_shape=jax.ShapeDtypeStruct((wide * groups, rows, cols), F32),
        in_specs=[SMEM_SPEC] + [VMEM_SPEC] * wide + [HBM_SPEC, ANY_SPEC],
        out_specs=VMEM_SPEC,
        scratch_shapes=[pltpu.VMEM((wide, depth // wide, cols), BF16), pltpu.SemaphoreType.DMA((wide,))],
        compiler_params=params(OUT_MIB),
        cost_estimate=cost(2 * rows * depth * cols, 2 * depth * cols),
        name="out_proj",
    )(me, *sent, weight, after)


def out_scale_kernel(me_ref, made_ref, *refs, wide, narrow, groups, group_span):
    squares, outs, chunks = refs[:narrow], refs[narrow : 2 * narrow], refs[-1]
    summed = summed_refs(squares)
    lane = iota(summed.shape, 1)
    total = None
    for mask in range(wide):
        owner = me_ref[0] ^ mask
        for g in range(groups):
            low = (owner // group_span * group_span) * groups + g
            mine = (lane >= low) & (lane < low + (group_span - 1) * groups + 1)
            group_sum = jnp.sum(jnp.where(mine, summed, 0.0), axis=1, keepdims=True)
            inverse = lax.rsqrt(group_sum / (HEADS // NGROUPS * HEAD_DIM) + EPSILON)
            scaled = made_ref[mask * groups + g] * inverse
            total = scaled if total is None else total + scaled
    cols = total.shape[1] // narrow
    for n in range(narrow):
        chunks[n] = total[:, n * cols : (n + 1) * cols].astype(BF16)
    for mask in range(narrow):
        outs[mask][...] = chunks[me_ref[1] ^ mask]


def out_scale(me, made, squares, wide, groups, group_span):
    narrow = len(squares)
    _, rows, cols = made.shape
    return pl.pallas_call(
        functools.partial(out_scale_kernel, wide=wide, narrow=narrow, groups=groups, group_span=group_span),
        out_shape=[jax.ShapeDtypeStruct((rows, cols // narrow), BF16)] * narrow,
        in_specs=[SMEM_SPEC] + [VMEM_SPEC] * (narrow + 1),
        out_specs=[VMEM_SPEC] * narrow,
        scratch_shapes=[pltpu.VMEM((narrow, rows, cols // narrow), BF16)],
        compiler_params=params(8),
        cost_estimate=cost(4 * made.size, 4 * made.size),
        name="out_scale",
    )(me, made, *squares)


def shards(
    inputs,
    xz_weight,
    bc_weight,
    dt_weight,
    conv_x_weight,
    conv_x_bias,
    conv_bc_weight,
    conv_bc_bias,
    conv_x_state,
    conv_bc_state,
    dt_bias,
    a_log,
    d_skip,
    norm_weight,
    out_weight,
    ssm_state,
):
    seqs = inputs.shape[0]
    feats = inputs.shape[2]
    heads = dt_weight.shape[1]
    wide = lax.axis_size("wide")
    narrow = lax.axis_size("narrow")
    chan = HEAD_DIM // narrow
    width = heads * chan
    half = -(-seqs // 8) * 8
    groups = max(NGROUPS // wide, 1)
    group_span = max(wide // NGROUPS, 1)
    me = jnp.stack([lax.axis_index("wide"), lax.axis_index("narrow")]).astype(jnp.int32)

    blocks = xz_weight.shape[2] // LANES
    cut = blocks // 2
    state = ssm_state.reshape(seqs, width, STATE)
    given = (inputs, bc_weight, dt_weight.T)
    spread, mover, *chunks = proj(me, xz_weight, given, half, narrow, chan, 0, cut, True)
    early_parts = [chunks[0]] + [exchanged(chunks[mask], "narrow", mask) for mask in range(1, narrow)]
    history = conv_x_state.transpose(0, 1, 3, 2)
    given = (spread, mover, history, conv_x_weight.transpose(0, 2, 1), conv_x_bias.T, norm_weight.T, state)
    state, lanes, *chunks = proj(me, xz_weight, given, half, narrow, chan, cut, blocks - cut, False)
    late_parts = [chunks[0]] + [exchanged(chunks[mask], "narrow", mask) for mask in range(1, narrow)]

    conv, kept_bc, dt, early_done = bc_conv(
        early_parts, conv_bc_state.transpose(1, 0, 2), conv_bc_weight, conv_bc_bias.reshape(1, -1), chunks[0].shape[1]
    )
    for bit in range(group_span.bit_length() - 1):
        partner = exchanged(conv.astype(BF16), "wide", 1 << bit).astype(F32)
        is_lower = lax.axis_index("wide") // (1 << bit) % 2 == 0
        conv = jnp.where(
            is_lower, jnp.concatenate([conv, partner], axis=1), jnp.concatenate([partner, conv], axis=1)
        )

    read = state_read(conv, state, groups)

    sent, fresh, scale, decay = readout(
        early_done,
        late_parts,
        lanes,
        read,
        conv,
        dt,
        jnp.stack([dt_bias, a_log, d_skip]),
        groups,
        chan,
    )

    gathered = from_all(sent, "wide")
    early = seqs * 3 // 5
    new_state, left, decays = state_write((scale, decay), conv, state, groups, heads, 0, early)
    squares = all_squares(me, gathered, groups, left)
    square_list = from_all(squares, "narrow")
    made = out_proj(me, gathered, out_weight.reshape(-1, out_weight.shape[2]), groups, squares)
    out_chunks = out_scale(me, made, square_list, wide, groups, group_span)
    new_state, _ = state_write(
        (left, decays), conv, state, groups, heads, early, seqs - early, new_state, out_chunks[0]
    )
    out_sum = out_chunks[0].astype(F32)
    for mask in range(1, narrow):
        out_sum = out_sum + exchanged(out_chunks[mask], "narrow", mask).astype(F32)
    layer_out = out_sum.astype(BF16).reshape(2, half, -1)[:, :seqs].transpose(1, 0, 2)

    new_conv_x = kept_channels(history, fresh).transpose(0, 1, 3, 2)
    return (layer_out, new_state.reshape(ssm_state.shape), new_conv_x, kept_bc.transpose(1, 0, 2))


def solution(mesh):
    return jax.shard_map(
        shards,
        mesh=mesh,
        in_specs=(
            P("groups", None, "narrow"),
            P("narrow", None, "wide"),
            P("narrow", "wide"),
            P("narrow", "wide"),
            P(None, "wide", "narrow"),
            P("wide", "narrow"),
            P(None, "wide"),
            P("wide"),
            P("groups", None, "wide", "narrow"),
            P("groups", None, "wide"),
            P("wide"),
            P("wide"),
            P("wide"),
            P("wide", "narrow"),
            P(None, "narrow", "wide"),
            P("groups", "wide", "narrow", None),
        ),
        out_specs=(
            P("groups", None, ("wide", "narrow")),
            P("groups", "wide", "narrow", None),
            P("groups", None, "wide", "narrow"),
            P("groups", None, "wide"),
        ),
        check_vma=False,
    )
```

time: 104 us -> 75.9 us (0.73)
  local copies, waits for them, and re-layouts: 28.9 us -> 2.88 us
  waiting for transfers between devices: 17.2 us -> 4.04 us
  Pallas kernels: 41.5 us -> 53.3 us
    unnamed x36 -> x29, local copies, waits for them, and re-layouts: 25.3 us -> 2.87 us
    ppermute x15, waiting for transfers between devices: 17.2 us -> 4.04 us  [exchanged(): lax.ppermute(value, axis, [(i, i ^ mask) for i in range(lax.axis_size(axi...]
    pallas_call x7 -> x10, Pallas kernels: 40.7 us -> 52.5 us  [the longest x2 27.4 us: proj(): pl.pallas_call(functools.partial(proj_kernel, slots=slots, first=first, n...]
    reshape x5 -> x0, local copies, waits for them, and re-layouts: 2.19 us -> none  [the longest x1 1.63 us: shards(): history = rows_of(conv_x_state.reshape(seqs, 3, width).transpose(1, 0, 2))]
    transpose x2 -> x0, local copies, waits for them, and re-layouts: 1.23 us -> none  [shards(): fresh = fresh.reshape(2, half, heads, chan)[:, :seqs].transpose(1, 0, 2, 3)]
  transfers between devices with their start and end apart: 15 -> 15, of which waited for: 4 -> 2; matrix products, arithmetic and copies ran while one was open for 6% -> 0% of each run, Pallas kernels for 34% -> 49%
where the time goes in v2:
time: 75.9 us; the launch traced here: 75.7 us
  Pallas kernels  53.3 us (70%)
  starting transfers between devices  13.8 us (18%)
  waiting for transfers between devices  4.04 us (5%)
  local copies, waits for them, and re-layouts  2.88 us (4%)
  between operations  0.95 us (1%)
    pallas_call x2, Pallas kernels, proj(): pl.pallas_call(functools.partial(proj_kernel, slots=slots, first=first, n...  27.4 us
    ppermute x15, starting transfers between devices, exchanged(): lax.ppermute(value, axis, [(i, i ^ mask) for i in range(lax.axis_size(axi...  13.8 us
    pallas_call x2, Pallas kernels, state_write(): pl.pallas_call(functools.partial(state_write_kernel, groups=groups, heads...  10.9 us
    pallas_call x1, Pallas kernels, out_proj(): pl.pallas_call(functools.partial(out_proj_kernel, wide=wide, groups=group...  7.27 us
    ppermute x15, waiting for transfers between devices, exchanged(): lax.ppermute(value, axis, [(i, i ^ mask) for i in range(lax.axis_size(axi...  4.04 us
    unnamed x29, local copies, waits for them, and re-layouts  2.87 us
    pallas_call x1, Pallas kernels, state_read(): pl.pallas_call(functools.partial(state_read_kernel, groups=groups), out_s...  2.83 us
    pallas_call x1, Pallas kernels, kept_channels(): pl.pallas_call(kept_channels_kernel, out_shape=jax.ShapeDtypeStruct(histo...  1.65 us
  transfers between devices with their start and end apart: 15, of which 2 were waited for; matrix products, arithmetic and copies ran while one was open for 0% of the time, Pallas kernels for 49%

profile of v2, /device:TPU:0, one launch (start us, length us, event | category | flops | bytes accessed | tf_op | source)
XLA Modules:
  0.0 75.7 jit_solution(18439940980081294967)
XLA Ops:
  0.7 0.7 pad_add_fusion.refs_0_.me_ref
  1.3 13.8 %proj_small.1 = (bf16[96,4096]{1,0:T(8,128)(2,1)}, bf16[512,512]{1,0:T(8,128)(2,1)}, bf16[96,1152]{1,0:T(8,128)(2,1)}, bf16[96,1152]{1,0:T(8,128)(2,1)}, bf16[96...) custom-call(s32[2]{0:T(128)} %pad_add_fusion.refs_0_.me_ref, bf16[2048,32,2,128]{3,2,1,0:T(2,128)(2,1)} %bitcast.30, ...), custom_call_target="tpu_custom_call" | custom-call | flops 1019215872 | bytes 21233664 | tf_op jit(solution)/shard_map/proj_small/pallas_call | solution.py:259
  15.2 0.5 collective-permute-start
  15.7 2.6 %collective-permute-start.1 = (bf16[96,1152]{1,0:T(8,128)(2,1)}, bf16[96,1152]{1,0:T(8,128)(2,1)S(1)}, u32[]{:S(2)}, u32[]{:S(2)}) collective-permute-start(bf16[96,1152]{1,0:T(8,128)(2,1)} %get-tuple-element.34), channel_id=1, source_target_pairs={{0,2},{1,3},{2,0},{3,1},{4,6},{5,7},{6,4},{7,5},{8,10},{9,11},{10,... | collective-permute-start | bytes 663560 | tf_op jit(solution)/shard_map/ppermute | solution.py:33
  18.2 0.1 collective-permute-start.2
  18.4 1.1 %copy-done.1 = bf16[96,4096]{1,0:T(8,128)(2,1)S(1)} copy-done((bf16[96,4096]{1,0:T(8,128)(2,1)S(1)}, bf16[96,4096]{1,0:T(8,128)(2,1)}, u32[]{:S(2)}) %copy-start.1) | copy-done | bytes 786456
  19.5 1.0 %copy-done.2 = bf16[512,512]{1,0:T(8,128)(2,1)S(1)} copy-done((bf16[512,512]{1,0:T(8,128)(2,1)S(1)}, bf16[512,512]{1,0:T(8,128)(2,1)}, u32[]{:S(2)}) %copy-start.2) | copy-done | bytes 524312
  20.6 13.6 %proj.1 = (f32[20,1024,256]{2,1,0:T(8,128)S(1)}, bf16[80,1024]{1,0:T(8,128)(2,1)S(1)}, bf16[96,512]{1,0:T(8,128)(2,1)S(1)}, bf16[96,512]{1,0:T(8,128)(2,1)S(1)},...) custom-call(s32[2]{0:T(128)S(1)} %copy-done.6, bf16[2048,32,2,128]{3,2,1,0:T(2,128)(2,1)} %bitcast.31, ...), custom_call_target="tpu_custom_call" | custom-call | flops 1811939328 | bytes 37748736 | tf_op jit(solution)/shard_map/proj/pallas_call | solution.py:259
  34.2 0.2 collective-permute-start.3
  34.4 1.9 %collective-permute-start.4 = (bf16[96,512]{1,0:T(8,128)(2,1)S(1)}, bf16[96,512]{1,0:T(8,128)(2,1)S(1)}, u32[]{:S(2)}, u32[]{:S(2)}) collective-permute-start(bf16[96,512]{1,0:T(8,128)(2,1)S(1)} %get-tuple-element.41), channel_id=1, source_target_pairs={{0,2},{1,3},{2,0},{3,1},{4,6},{5,7},{6,4},{7,5},{8,10},{9,11},{10,... | collective-permute-start | bytes 294920 | tf_op jit(solution)/shard_map/ppermute | solution.py:33
  36.4 0.1 collective-permute-start.5
  36.5 0.8 %bc_conv.1 = (f32[48,1024]{1,0:T(8,128)S(1)}, bf16[3,20,1024]{2,1,0:T(8,128)(2,1)}, f32[48,128]{1,0:T(8,128)S(1)}, bf16[96,512]{1,0:T(8,128)(2,1)S(1)}) custom-call(bf16[96,1152]{1,0:T(8,128)(2,1)S(1)} %copy-done.3, bf16[96,1152]{1,0:T(8,128)(2,1)S(1)} %collective-permute-done.refs_1_, bf16[96,1152]{1,0:T(8,128)(2,1)S(1)} %collective-permute-done.1.refs_2_, ...), custom_call_target="tpu_custom_call" | custom-call | flops 2949120 | bytes 786432 | tf_op jit(solution)/shard_map/bc_conv/pallas_call | solution.py:314
  37.4 2.8 %state_read.1.refs_6_ = f32[48,1024]{1,0:T(8,128)S(1)} custom-call(f32[48,1024]{1,0:T(8,128)S(1)} %get-tuple-element.44.bc_ref.refs_7_.refs_2_, f32[20,1024,256]{2,1,0:T(8,128)S(1)} %get-tuple-element.45.state_ref.refs_3_), custom_call_target="tpu_custom_call" | custom-call | flops 20971520 | bytes 20971520 | tf_op jit(solution)/shard_map/state_read/pallas_call | solution.py:347
  40.2 0.0 collective-permute-done.4.refs_3_
  40.2 1.3 %collective-permute-done.5.refs_4_ = bf16[96,512]{1,0:T(8,128)(2,1)S(1)} collective-permute-done((bf16[96,512]{1,0:T(8,128)(2,1)S(1)}, bf16[96,512]{1,0:T(8,128)(2,1)S(1)}, u32[]{:S(2)}, u32[]{:S(2)}) %collective-permute-start.5) | collective-permute-done | bytes 98336 | tf_op jit(solution)/shard_map/ppermute | solution.py:33
  41.6 0.7 readout.1
  42.2 1.6 %collective-permute-start.6 = (bf16[48,1152]{1,0:T(8,128)(2,1)S(1)}, bf16[48,1152]{1,0:T(8,128)(2,1)S(1)}, u32[]{:S(2)}, u32[]{:S(2)}) collective-permute-start(bf16[48,1152]{1,0:T(8,128)(2,1)S(1)} %get-tuple-element.47.refs_0_), channel_id=1, source_target_pairs={{0,4},{4,0},{8,12},{12,8},{1,5},{5,1},{9,13},{13,9},{2,6},{6,2},{1... | collective-permute-start | bytes 331784 | tf_op jit(solution)/shard_map/ppermute | solution.py:33
  43.8 2.6 %collective-permute-start.7 = (bf16[48,1152]{1,0:T(8,128)(2,1)S(1)}, bf16[48,1152]{1,0:T(8,128)(2,1)S(1)}, u32[]{:S(2)}, u32[]{:S(2)}) collective-permute-start(bf16[48,1152]{1,0:T(8,128)(2,1)S(1)} %get-tuple-element.47.refs_0_), channel_id=1, source_target_pairs={{0,8},{4,12},{8,0},{12,4},{1,9},{5,13},{9,1},{13,5},{2,10},{6,14},... | collective-permute-start | bytes 331784 | tf_op jit(solution)/shard_map/ppermute | solution.py:33
  46.4 0.3 collective-permute-start.8
  46.7 6.0 %state_write.2 = (f32[20,1024,256]{2,1,0:T(8,128)}, bf16[1024,256]{1,0:T(8,128)(2,1)S(1)}, f32[1280,128]{1,0:T(8,128)S(1)}) custom-call(f32[48,1024]{1,0:T(8,128)S(1)} %get-tuple-element.48.refs_0_, f32[24,64]{1,0:T(8,128)S(1)} %get-tuple-element.49.refs_1_, f32[48,1024]{1,0:T(8,128)S(1)} %get-tuple-element.44.bc_ref.refs_7_.refs_2_, ...), custom_call_target="tpu_custom_call" | custom-call | flops 12582912 | bytes 25165824 | tf_op jit(solution)/shard_map/state_write/pallas_call | solution.py:519
  52.8 2.6 %collective-permute-done.7.refs_2_ = bf16[48,1152]{1,0:T(8,128)(2,1)S(1)} collective-permute-done((bf16[48,1152]{1,0:T(8,128)(2,1)S(1)}, bf16[48,1152]{1,0:T(8,128)(2,1)S(1)}, u32[]{:S(2)}, u32[]{:S(2)}) %collective-permute-start.7) | collective-permute-done | bytes 110624 | tf_op jit(solution)/shard_map/ppermute | solution.py:33
  55.4 0.7 all_squares.1.refs_5_.refs_0_
  56.1 0.1 collective-permute-start.9
  56.2 1.1 %collective-permute-start.10 = (f32[48,128]{1,0:T(8,128)S(1)}, f32[48,128]{1,0:T(8,128)S(1)}, u32[]{:S(2)}, u32[]{:S(2)}) collective-permute-start(f32[48,128]{1,0:T(8,128)S(1)} %all_squares.1.refs_5_.refs_0_), channel_id=1, source_target_pairs={{0,2},{1,3},{2,0},{3,1},{4,6},{5,7},{6,4},{7,5},{8,10},{9,11},{10,... | collective-permute-start | bytes 73736 | tf_op jit(solution)/shard_map/ppermute | solution.py:33
  57.3 0.8 %collective-permute-start.11 = (f32[48,128]{1,0:T(8,128)S(1)}, f32[48,128]{1,0:T(8,128)S(1)}, u32[]{:S(2)}, u32[]{:S(2)}) collective-permute-start(f32[48,128]{1,0:T(8,128)S(1)} %all_squares.1.refs_5_.refs_0_), channel_id=1, source_target_pairs={{0,3},{1,2},{2,1},{3,0},{4,7},{5,6},{6,5},{7,4},{8,11},{9,10},{10,... | collective-permute-start | bytes 73736 | tf_op jit(solution)/shard_map/ppermute | solution.py:33
  58.1 7.3 %out_proj.1.made_ref = f32[8,48,2048]{2,1,0:T(8,128)S(1)} custom-call(s32[2]{0:T(128)S(1)} %copy-done.6, bf16[48,1152]{1,0:T(8,128)(2,1)S(1)} %get-tuple-element.47.refs_0_, bf16[48,1152]{1,0:T(8,128)(2,1)S(1)} %collective-permute-done.6.refs_1_, bf16[48,1152]{1,0:T(8,128)(2,1)S(1)} %collective-permute-done.7.refs_2_, ...), custom_call_target="tpu_custom_call" | custom-call | flops 805306368 | bytes 16777216 | tf_op jit(solution)/shard_map/out_proj/pallas_call | solution.py:586
  65.4 1.0 %out_scale.1 = (bf16[48,512]{1,0:T(8,128)(2,1)S(1)}, bf16[48,512]{1,0:T(8,128)(2,1)S(1)}, bf16[48,512]{1,0:T(8,128)(2,1)S(1)}, bf16[48,512]{1,0:T(8,128)(2,1)S(1)}) custom-call(s32[2]{0:T(128)S(1)} %copy-done.6, f32[8,48,2048]{2,1,0:T(8,128)S(1)} %out_proj.1.made_ref, f32[48,128]{1,0:T(8,128)S(1)} %all_squares.1.refs_5_.refs_0_, ...), custom_call_target="tpu_custom_call" | custom-call | flops 3145728 | bytes 3145728 | tf_op jit(solution)/shard_map/out_scale/pallas_call | solution.py:622
  66.4 1.0 %collective-permute-start.14 = (bf16[48,512]{1,0:T(8,128)(2,1)S(1)}, bf16[48,512]{1,0:T(8,128)(2,1)S(1)}, u32[]{:S(2)}, u32[]{:S(2)}) collective-permute-start(bf16[48,512]{1,0:T(8,128)(2,1)S(1)} %get-tuple-element.54), channel_id=1, source_target_pairs={{0,3},{1,2},{2,1},{3,0},{4,7},{5,6},{6,5},{7,4},{8,11},{9,10},{10,... | collective-permute-start | bytes 147464 | tf_op jit(solution)/shard_map/ppermute | solution.py:33
  67.4 1.0 %collective-permute-start.13 = (bf16[48,512]{1,0:T(8,128)(2,1)S(1)}, bf16[48,512]{1,0:T(8,128)(2,1)S(1)}, u32[]{:S(2)}, u32[]{:S(2)}) collective-permute-start(bf16[48,512]{1,0:T(8,128)(2,1)S(1)} %get-tuple-element.53), channel_id=1, source_target_pairs={{0,2},{1,3},{2,0},{3,1},{4,6},{5,7},{6,4},{7,5},{8,10},{9,11},{10,... | collective-permute-start | bytes 147464 | tf_op jit(solution)/shard_map/ppermute | solution.py:33
  68.4 1.6 %kept_channels.1 = bf16[20,3,16,64]{3,2,1,0:T(8,128)(2,1)} custom-call(bf16[20,3,16,64]{3,2,1,0:T(8,128)(2,1)S(1)} %bitcast.25, bf16[48,1024]{1,0:T(8,128)(2,1)S(1)} %get-tuple-element.58.fresh_ref), custom_call_target="tpu_custom_call" | custom-call | flops 4915200 | bytes 196608 | tf_op jit(solution)/shard_map/kept_channels/pallas_call | solution.py:97
  70.1 4.9 %state_write.3 = (f32[20,1024,256]{2,1,0:T(8,128)}, f32[8,128]{1,0:T(8,128)}) custom-call(bf16[1024,256]{1,0:T(8,128)(2,1)S(1)} %get-tuple-element.50.refs_4_.refs_0_, f32[1280,128]{1,0:T(8,128)S(1)} %get-tuple-element.55.refs_1_, f32[48,1024]{1,0:T(8,128)S(1)} %get-tuple-element.44.bc_ref.refs_7_.refs_2_, ...), custom_call_target="tpu_custom_call", output_to_operand_aliasing={{0}: (4, {})} | custom-call | flops 8388608 | bytes 16777216 | tf_op jit(solution)/shard_map/state_write/pallas_call | solution.py:519
  75.0 0.6 copy.24
  (42 shorter events, 0.1 us)
Async XLA Ops:
  0.6 17.7 %copy-start = (bf16[20,3,64,16]{2,3,1,0:T(8,128)(2,1)S(1)}, bf16[20,3,64,16]{2,3,1,0:T(8,128)(2,1)}, u32[]{:S(2)}) copy-start(bf16[20,3,64,16]{2,3,1,0:T(8,128)(2,1)} %param.24) | copy-start | bytes 368644
  0.6 17.7 %copy-start.5 = (bf16[4,64,16]{1,2,0:T(8,128)(2,1)S(1)}, bf16[4,64,16]{1,2,0:T(8,128)(2,1)}, u32[]{:S(2)}) copy-start(bf16[4,64,16]{1,2,0:T(8,128)(2,1)} %param.20) | copy-start | bytes 24580
  0.7 17.7 %copy-start.8 = (bf16[64,16]{0,1:T(8,128)(2,1)S(1)}, bf16[64,16]{0,1:T(8,128)(2,1)}, u32[]{:S(2)}) copy-start(bf16[64,16]{0,1:T(8,128)(2,1)} %param.21) | copy-start | bytes 6148
  0.7 17.7 %copy-start.9 = (bf16[64,16]{0,1:T(8,128)(2,1)S(1)}, bf16[64,16]{0,1:T(8,128)(2,1)}, u32[]{:S(2)}) copy-start(bf16[64,16]{0,1:T(8,128)(2,1)} %param.29) | copy-start | bytes 6148
  1.3 17.0 %copy-start.6 = (s32[2]{0:T(128)S(1)}, s32[2]{0:T(128)}, u32[]{:S(2)}) copy-start(s32[2]{0:T(128)} %pad_add_fusion.refs_0_.me_ref) | copy-start | bytes 28
  15.2 21.2 %collective-permute-start = (bf16[96,1152]{1,0:T(8,128)(2,1)}, bf16[96,1152]{1,0:T(8,128)(2,1)S(1)}, u32[]{:S(2)}, u32[]{:S(2)}) collective-permute-start(bf16[96,1152]{1,0:T(8,128)(2,1)} %get-tuple-element.33), channel_id=1, source_target_pairs={{0,1},{1,0},{2,3},{3,2},{4,5},{5,4},{6,7},{7,6},{8,9},{9,8},{10,11... | collective-permute-start | bytes 663560 | tf_op jit(solution)/shard_map/ppermute | solution.py:33
  15.7 20.8 %collective-permute-start.1 = (bf16[96,1152]{1,0:T(8,128)(2,1)}, bf16[96,1152]{1,0:T(8,128)(2,1)S(1)}, u32[]{:S(2)}, u32[]{:S(2)}) collective-permute-start(bf16[96,1152]{1,0:T(8,128)(2,1)} %get-tuple-element.34), channel_id=1, source_target_pairs={{0,2},{1,3},{2,0},{3,1},{4,6},{5,7},{6,4},{7,5},{8,10},{9,11},{10,... | collective-permute-start | bytes 663560 | tf_op jit(solution)/shard_map/ppermute | solution.py:33
  18.2 18.2 %collective-permute-start.2 = (bf16[96,1152]{1,0:T(8,128)(2,1)}, bf16[96,1152]{1,0:T(8,128)(2,1)S(1)}, u32[]{:S(2)}, u32[]{:S(2)}) collective-permute-start(bf16[96,1152]{1,0:T(8,128)(2,1)} %get-tuple-element.35), channel_id=1, source_target_pairs={{0,3},{1,2},{2,1},{3,0},{4,7},{5,6},{6,5},{7,4},{8,11},{9,10},{10,... | collective-permute-start | bytes 663560 | tf_op jit(solution)/shard_map/ppermute | solution.py:33
  18.3 1.1 %copy-start.1 = (bf16[96,4096]{1,0:T(8,128)(2,1)S(1)}, bf16[96,4096]{1,0:T(8,128)(2,1)}, u32[]{:S(2)}) copy-start(bf16[96,4096]{1,0:T(8,128)(2,1)} %get-tuple-element.37.refs_2_) | copy-start | bytes 2359300
  19.5 1.0 %copy-start.2 = (bf16[512,512]{1,0:T(8,128)(2,1)S(1)}, bf16[512,512]{1,0:T(8,128)(2,1)}, u32[]{:S(2)}) copy-start(bf16[512,512]{1,0:T(8,128)(2,1)} %get-tuple-element.38.refs_3_) | copy-start | bytes 1572868
  20.5 15.8 %copy-start.10 = (bf16[1024]{0:T(1024)(128)(2,1)S(1)}, bf16[1024]{0:T(1024)(128)(2,1)}, u32[]{:S(2)}) copy-start(bf16[1024]{0:T(1024)(128)(2,1)} %param.23) | copy-start | bytes 6148
  20.5 15.9 %copy-start.11 = (f32[64]{0:T(128)S(1)}, f32[64]{0:T(128)}, u32[]{:S(2)}) copy-start(f32[64]{0:T(128)} %param.28) | copy-start | bytes 772
  20.5 15.9 %copy-start.12 = (f32[64]{0:T(128)S(1)}, f32[64]{0:T(128)}, u32[]{:S(2)}) copy-start(f32[64]{0:T(128)} %param.27) | copy-start | bytes 772
  20.5 15.9 %copy-start.13 = (f32[64]{0:T(128)S(1)}, f32[64]{0:T(128)}, u32[]{:S(2)}) copy-start(f32[64]{0:T(128)} %param.26) | copy-start | bytes 772
  20.5 16.0 %copy-start.3 = (bf16[96,1152]{1,0:T(8,128)(2,1)S(1)}, bf16[96,1152]{1,0:T(8,128)(2,1)}, u32[]{:S(2)}) copy-start(bf16[96,1152]{1,0:T(8,128)(2,1)} %get-tuple-element.32.refs_0_) | copy-start | bytes 663556
  20.5 16.0 %copy-start.4 = (bf16[20,3,1024]{2,0,1:T(8,128)(2,1)S(1)}, bf16[20,3,1024]{2,0,1:T(8,128)(2,1)}, u32[]{:S(2)}) copy-start(bf16[20,3,1024]{2,0,1:T(8,128)(2,1)} %param.25) | copy-start | bytes 368644
  20.6 16.0 %copy-start.7 = (bf16[4,1024]{1,0:T(4,128)(2,1)S(1)}, bf16[4,1024]{1,0:T(4,128)(2,1)}, u32[]{:S(2)}) copy-start(bf16[4,1024]{1,0:T(4,128)(2,1)} %refs_5_.1) | copy-start | bytes 24580
  34.2 6.0 %collective-permute-start.3 = (bf16[96,512]{1,0:T(8,128)(2,1)S(1)}, bf16[96,512]{1,0:T(8,128)(2,1)S(1)}, u32[]{:S(2)}, u32[]{:S(2)}) collective-permute-start(bf16[96,512]{1,0:T(8,128)(2,1)S(1)} %get-tuple-element.40), channel_id=1, source_target_pairs={{0,1},{1,0},{2,3},{3,2},{4,5},{5,4},{6,7},{7,6},{8,9},{9,8},{10,11... | collective-permute-start | bytes 294920 | tf_op jit(solution)/shard_map/ppermute | solution.py:33
  34.4 5.8 %collective-permute-start.4 = (bf16[96,512]{1,0:T(8,128)(2,1)S(1)}, bf16[96,512]{1,0:T(8,128)(2,1)S(1)}, u32[]{:S(2)}, u32[]{:S(2)}) collective-permute-start(bf16[96,512]{1,0:T(8,128)(2,1)S(1)} %get-tuple-element.41), channel_id=1, source_target_pairs={{0,2},{1,3},{2,0},{3,1},{4,6},{5,7},{6,4},{7,5},{8,10},{9,11},{10,... | collective-permute-start | bytes 294920 | tf_op jit(solution)/shard_map/ppermute | solution.py:33
  36.4 5.2 %collective-permute-start.5 = (bf16[96,512]{1,0:T(8,128)(2,1)S(1)}, bf16[96,512]{1,0:T(8,128)(2,1)S(1)}, u32[]{:S(2)}, u32[]{:S(2)}) collective-permute-start(bf16[96,512]{1,0:T(8,128)(2,1)S(1)} %get-tuple-element.42), channel_id=1, source_target_pairs={{0,3},{1,2},{2,1},{3,0},{4,7},{5,6},{6,5},{7,4},{8,11},{9,10},{10,... | collective-permute-start | bytes 294920 | tf_op jit(solution)/shard_map/ppermute | solution.py:33
  42.2 10.5 %collective-permute-start.6 = (bf16[48,1152]{1,0:T(8,128)(2,1)S(1)}, bf16[48,1152]{1,0:T(8,128)(2,1)S(1)}, u32[]{:S(2)}, u32[]{:S(2)}) collective-permute-start(bf16[48,1152]{1,0:T(8,128)(2,1)S(1)} %get-tuple-element.47.refs_0_), channel_id=1, source_target_pairs={{0,4},{4,0},{8,12},{12,8},{1,5},{5,1},{9,13},{13,9},{2,6},{6,2},{1... | collective-permute-start | bytes 331784 | tf_op jit(solution)/shard_map/ppermute | solution.py:33
  43.8 11.6 %collective-permute-start.7 = (bf16[48,1152]{1,0:T(8,128)(2,1)S(1)}, bf16[48,1152]{1,0:T(8,128)(2,1)S(1)}, u32[]{:S(2)}, u32[]{:S(2)}) collective-permute-start(bf16[48,1152]{1,0:T(8,128)(2,1)S(1)} %get-tuple-element.47.refs_0_), channel_id=1, source_target_pairs={{0,8},{4,12},{8,0},{12,4},{1,9},{5,13},{9,1},{13,5},{2,10},{6,14},... | collective-permute-start | bytes 331784 | tf_op jit(solution)/shard_map/ppermute | solution.py:33
  46.4 9.0 %collective-permute-start.8 = (bf16[48,1152]{1,0:T(8,128)(2,1)S(1)}, bf16[48,1152]{1,0:T(8,128)(2,1)S(1)}, u32[]{:S(2)}, u32[]{:S(2)}) collective-permute-start(bf16[48,1152]{1,0:T(8,128)(2,1)S(1)} %get-tuple-element.47.refs_0_), channel_id=1, source_target_pairs={{0,12},{4,8},{8,4},{12,0},{1,13},{5,9},{9,5},{13,1},{2,14},{6,10},... | collective-permute-start | bytes 331784 | tf_op jit(solution)/shard_map/ppermute | solution.py:33
  56.1 9.2 %collective-permute-start.9 = (f32[48,128]{1,0:T(8,128)S(1)}, f32[48,128]{1,0:T(8,128)S(1)}, u32[]{:S(2)}, u32[]{:S(2)}) collective-permute-start(f32[48,128]{1,0:T(8,128)S(1)} %all_squares.1.refs_5_.refs_0_), channel_id=1, source_target_pairs={{0,1},{1,0},{2,3},{3,2},{4,5},{5,4},{6,7},{7,6},{8,9},{9,8},{10,11... | collective-permute-start | bytes 73736 | tf_op jit(solution)/shard_map/ppermute | solution.py:33
  56.2 9.2 %collective-permute-start.10 = (f32[48,128]{1,0:T(8,128)S(1)}, f32[48,128]{1,0:T(8,128)S(1)}, u32[]{:S(2)}, u32[]{:S(2)}) collective-permute-start(f32[48,128]{1,0:T(8,128)S(1)} %all_squares.1.refs_5_.refs_0_), channel_id=1, source_target_pairs={{0,2},{1,3},{2,0},{3,1},{4,6},{5,7},{6,4},{7,5},{8,10},{9,11},{10,... | collective-permute-start | bytes 73736 | tf_op jit(solution)/shard_map/ppermute | solution.py:33
  57.3 8.1 %collective-permute-start.11 = (f32[48,128]{1,0:T(8,128)S(1)}, f32[48,128]{1,0:T(8,128)S(1)}, u32[]{:S(2)}, u32[]{:S(2)}) collective-permute-start(f32[48,128]{1,0:T(8,128)S(1)} %all_squares.1.refs_5_.refs_0_), channel_id=1, source_target_pairs={{0,3},{1,2},{2,1},{3,0},{4,7},{5,6},{6,5},{7,4},{8,11},{9,10},{10,... | collective-permute-start | bytes 73736 | tf_op jit(solution)/shard_map/ppermute | solution.py:33
  66.4 8.6 %collective-permute-start.14 = (bf16[48,512]{1,0:T(8,128)(2,1)S(1)}, bf16[48,512]{1,0:T(8,128)(2,1)S(1)}, u32[]{:S(2)}, u32[]{:S(2)}) collective-permute-start(bf16[48,512]{1,0:T(8,128)(2,1)S(1)} %get-tuple-element.54), channel_id=1, source_target_pairs={{0,3},{1,2},{2,1},{3,0},{4,7},{5,6},{6,5},{7,4},{8,11},{9,10},{10,... | collective-permute-start | bytes 147464 | tf_op jit(solution)/shard_map/ppermute | solution.py:33
  67.4 7.5 %collective-permute-start.13 = (bf16[48,512]{1,0:T(8,128)(2,1)S(1)}, bf16[48,512]{1,0:T(8,128)(2,1)S(1)}, u32[]{:S(2)}, u32[]{:S(2)}) collective-permute-start(bf16[48,512]{1,0:T(8,128)(2,1)S(1)} %get-tuple-element.53), channel_id=1, source_target_pairs={{0,2},{1,3},{2,0},{3,1},{4,6},{5,7},{6,4},{7,5},{8,10},{9,11},{10,... | collective-permute-start | bytes 147464 | tf_op jit(solution)/shard_map/ppermute | solution.py:33
  68.4 6.5 %collective-permute-start.12 = (bf16[48,512]{1,0:T(8,128)(2,1)S(1)}, bf16[48,512]{1,0:T(8,128)(2,1)S(1)}, u32[]{:S(2)}, u32[]{:S(2)}) collective-permute-start(bf16[48,512]{1,0:T(8,128)(2,1)S(1)} %get-tuple-element.52), channel_id=1, source_target_pairs={{0,1},{1,0},{2,3},{3,2},{4,5},{5,4},{6,7},{7,6},{8,9},{9,8},{10,11... | collective-permute-start | bytes 147464 | tf_op jit(solution)/shard_map/ppermute | solution.py:33

commit v3 on v2

--- a/solution.py
+++ b/solution.py
@@ -106,19 +106,18 @@
 
 
 def proj_kernel(*refs, slots, first, narrow, chan, half, small):
-    me_ref, w_ref = refs[:2]
+    me_ref, w_ref, x_ref = refs[:3]
     if small:
-        x_ref, bc_ref, dt_ref, spread, mover = refs[2:7]
-        x_held, bc_held, dt_held, x_sem, bc_sem, dt_sem = refs[-6:]
-        refs = refs[7:-6]
+        bc_ref, dt_ref = refs[3:5]
+        bc_held, dt_held, bc_sem, dt_sem = refs[-4:]
+        refs = refs[5:-4]
     else:
-        spread, mover = refs[2:4]
-        channel_refs = refs[4:8]
-        later_ref, later, lanes_ref = refs[8:11]
+        channel_refs = refs[3:7]
+        later_ref, later, lanes_ref = refs[7:10]
         later_sem = refs[-1]
-        refs = refs[11:-1]
+        refs = refs[10:-1]
     outs = refs[:narrow]
-    held, flat, total, chunks, held_sem, flat_sem = refs[narrow:]
+    held, flat, x_held, spread, mover, total, chunks, held_sem, flat_sem, x_sem = refs[narrow:]
     feats = w_ref.shape[0]
     rows = spread.shape[0] // 2
     span = mover.shape[0]
@@ -143,11 +142,11 @@
     def later_copy(i):
         return pltpu.make_async_copy(later_ref.at[i], later.at[i], later_sem.at[i])
 
+    x_copy = pltpu.make_async_copy(x_ref, x_held, x_sem)
+    x_copy.start()
     if small:
-        x_copy = pltpu.make_async_copy(x_ref, x_held, x_sem)
         bc_copy = pltpu.make_async_copy(bc_ref, bc_held, bc_sem)
         dt_copy = pltpu.make_async_copy(dt_ref, dt_held, dt_sem)
-        x_copy.start()
     for i in range(min(slots, steps)):
         for copy in copies(i):
             copy.start()
@@ -155,29 +154,27 @@
         bc_copy.start()
         dt_copy.start()
 
-    if small:
-        x_copy.wait()
-        seqs, tokens, _ = x_held.shape
-        given = iota((rows, tokens * seqs), 1)
-        wanted = iota((rows, tokens * seqs), 0)
-        order = (given % tokens * half + given // tokens == wanted).astype(F32).astype(BF16)
-        x = jnp.dot(order, x_held[...].reshape(tokens * seqs, feats), preferred_element_type=F32)
-        x = x.astype(BF16)
-        piece = min(256, feats)
-        pieces = feats // piece
-        stacked = jnp.concatenate([x[:, i * piece : (i + 1) * piece] for i in range(pieces)], axis=0)
-        place = iota((piece, 2 * piece), 1) - 2 * iota((piece, 2 * piece), 0)
-        for z in range(2):
-            one_hot = (place == z).astype(F32).astype(BF16)
-            moved = jnp.dot(stacked, one_hot, preferred_element_type=F32).astype(BF16)
-            for i in range(pieces):
-                columns = slice(2 * i * piece, 2 * (i + 1) * piece)
-                spread[z * rows : (z + 1) * rows, columns] = moved[i * rows : (i + 1) * rows]
-        column = iota((span, span), 0)
-        target = (column % HEAD_DIM) // chan * (span // narrow) + column // HEAD_DIM * chan + column % chan
-        mover[...] = (target == iota((span, span), 1)).astype(F32).astype(BF16)
-
-    else:
+    x_copy.wait()
+    seqs, tokens, _ = x_held.shape
+    given = iota((rows, tokens * seqs), 1)
+    wanted = iota((rows, tokens * seqs), 0)
+    order = (given % tokens * half + given // tokens == wanted).astype(F32).astype(BF16)
+    x = jnp.dot(order, x_held[...].reshape(tokens * seqs, feats), preferred_element_type=F32)
+    x = x.astype(BF16)
+    piece = min(256, feats)
+    pieces = feats // piece
+    stacked = jnp.concatenate([x[:, i * piece : (i + 1) * piece] for i in range(pieces)], axis=0)
+    place = iota((piece, 2 * piece), 1) - 2 * iota((piece, 2 * piece), 0)
+    for z in range(2):
+        one_hot = (place == z).astype(F32).astype(BF16)
+        moved = jnp.dot(stacked, one_hot, preferred_element_type=F32).astype(BF16)
+        for i in range(pieces):
+            columns = slice(2 * i * piece, 2 * (i + 1) * piece)
+            spread[z * rows : (z + 1) * rows, columns] = moved[i * rows : (i + 1) * rows]
+    column = iota((span, span), 0)
+    target = (column % HEAD_DIM) // chan * (span // narrow) + column // HEAD_DIM * chan + column % chan
+    mover[...] = (target == iota((span, span), 1)).astype(F32).astype(BF16)
+    if not small:
         lanes_ref[...] = channel_lanes(channel_refs, half, lanes_ref.shape)
 
     def arrived(i):
@@ -221,35 +218,37 @@
         later_copy(j).wait()
 
 
-def proj(me, weight, given, half, narrow, chan, first, blocks, small, slots=4):
+def proj(me, weight, inputs, given, half, narrow, chan, first, blocks, small, slots):
     feats, _, cols = weight.shape
-    rows = 2 * half
+    rows = inputs.shape[1] * half
     pair = 2 if blocks % 2 == 0 else 1
+    slots = min(slots, blocks // pair)
+    span = min(narrow, blocks) * LANES
     by_block = weight.reshape(feats, 2, cols // LANES, LANES).transpose(0, 2, 1, 3)
     cols = blocks * LANES // narrow
     scratch = [
         pltpu.VMEM((slots, pair, feats, 2, LANES), BF16),
         pltpu.VMEM((2, pair * 2 * feats, LANES), BF16),
+        pltpu.VMEM(inputs.shape, BF16),
+        pltpu.VMEM((2 * rows, 2 * feats), BF16),
+        pltpu.VMEM((span, span), BF16),
         pltpu.VMEM((2 * rows, blocks * LANES), BF16),
         pltpu.VMEM((narrow, 2 * rows, blocks * LANES // narrow), BF16),
         pltpu.SemaphoreType.DMA((slots, pair)),
         pltpu.SemaphoreType.DMA((2,)),
+        pltpu.SemaphoreType.DMA,
     ]
     specs = [VMEM_SPEC] * len(given)
     nbytes = 4 * feats * blocks * LANES
     if small:
-        inputs, bc_weight, dt_weight_t = given
-        span = min(narrow, blocks) * LANES
-        out_shape = [
-            jax.ShapeDtypeStruct((2 * rows, 2 * feats), BF16),
-            jax.ShapeDtypeStruct((span, span), BF16),
-        ]
+        bc_weight, dt_weight_t = given
+        out_shape = []
         cols += -(-(bc_weight.shape[1] + dt_weight_t.shape[0]) // (2 * LANES)) * LANES
-        scratch += [pltpu.VMEM(value.shape, BF16) for value in given] + [pltpu.SemaphoreType.DMA] * 3
-        specs = [HBM_SPEC] * 3
+        scratch += [pltpu.VMEM(value.shape, BF16) for value in given] + [pltpu.SemaphoreType.DMA] * 2
+        specs = [HBM_SPEC] * 2
         nbytes += 2 * (bc_weight.size + dt_weight_t.size)
     else:
-        history, later = given[2], given[-1]
+        history, later = given[0], given[-1]
         specs[-1] = HBM_SPEC
         nbytes += later.size * later.dtype.itemsize
         scratch += [pltpu.SemaphoreType.DMA((later.shape[0],))]
@@ -261,13 +260,13 @@
             proj_kernel, slots=slots, first=first, narrow=narrow, chan=chan, half=half, small=small
         ),
         out_shape=out_shape,
-        in_specs=[SMEM_SPEC, HBM_SPEC] + specs,
+        in_specs=[SMEM_SPEC, HBM_SPEC, HBM_SPEC] + specs,
         out_specs=[VMEM_SPEC] * len(out_shape),
         scratch_shapes=scratch,
         compiler_params=params(PROJ_MIB if small else NEXT_PROJ_MIB),
         cost_estimate=cost(rows * nbytes, nbytes),
         name="proj_small" if small else "proj",
-    )(me, by_block, *given)
+    )(me, by_block, inputs, *given)
 
 
 def conv_pair(history, fresh, taps, offset):
@@ -564,16 +563,17 @@
     width = w_ref.shape[0] // wide
     span = width // groups
 
-    def copy(mask):
+    def copy(mask, g):
         owner = me_ref[0] ^ mask
-        rows = pl.ds(pl.multiple_of(owner * width, width), width)
-        return pltpu.make_async_copy(w_ref.at[rows], held.at[mask], sems.at[mask])
+        rows = pl.ds(pl.multiple_of(owner * width + g * span, span), span)
+        return pltpu.make_async_copy(w_ref.at[rows], held.at[mask, pl.ds(g * span, span)], sems.at[mask, g])
 
     for mask in range(wide):
-        copy(mask).start()
+        for g in range(groups):
+            copy(mask, g).start()
     for mask in range(wide):
-        copy(mask).wait()
         for g in range(groups):
+            copy(mask, g).wait()
             rows = slice(g * span, (g + 1) * span)
             product = jnp.dot(sent[mask][:, rows], held[mask, rows], preferred_element_type=F32)
             made_ref[mask * groups + g] = product
@@ -588,7 +588,7 @@
         out_shape=jax.ShapeDtypeStruct((wide * groups, rows, cols), F32),
         in_specs=[SMEM_SPEC] + [VMEM_SPEC] * wide + [HBM_SPEC, ANY_SPEC],
         out_specs=VMEM_SPEC,
-        scratch_shapes=[pltpu.VMEM((wide, depth // wide, cols), BF16), pltpu.SemaphoreType.DMA((wide,))],
+        scratch_shapes=[pltpu.VMEM((wide, depth // wide, cols), BF16), pltpu.SemaphoreType.DMA((wide, groups))],
         compiler_params=params(OUT_MIB),
         cost_estimate=cost(2 * rows * depth * cols, 2 * depth * cols),
         name="out_proj",
@@ -664,12 +664,12 @@
     blocks = xz_weight.shape[2] // LANES
     cut = blocks // 2
     state = ssm_state.reshape(seqs, width, STATE)
-    given = (inputs, bc_weight, dt_weight.T)
-    spread, mover, *chunks = proj(me, xz_weight, given, half, narrow, chan, 0, cut, True)
+    given = (bc_weight, dt_weight.T)
+    chunks = proj(me, xz_weight, inputs, given, half, narrow, chan, 0, cut, True, 3)
     early_parts = [chunks[0]] + [exchanged(chunks[mask], "narrow", mask) for mask in range(1, narrow)]
     history = conv_x_state.transpose(0, 1, 3, 2)
-    given = (spread, mover, history, conv_x_weight.transpose(0, 2, 1), conv_x_bias.T, norm_weight.T, state)
-    state, lanes, *chunks = proj(me, xz_weight, given, half, narrow, chan, cut, blocks - cut, False)
+    given = (history, conv_x_weight.transpose(0, 2, 1), conv_x_bias.T, norm_weight.T, state)
+    state, lanes, *chunks = proj(me, xz_weight, inputs, given, half, narrow, chan, cut, blocks - cut, False, 4)
     late_parts = [chunks[0]] + [exchanged(chunks[mask], "narrow", mask) for mask in range(1, narrow)]
 
     conv, kept_bc, dt, early_done = bc_conv(
@@ -697,7 +697,7 @@
     )
 
     gathered = from_all(sent, "wide")
-    early = seqs * 3 // 5
+    early = seqs * 4 // 5
     new_state, left, decays = state_write((scale, decay), conv, state, groups, heads, 0, early)
     squares = all_squares(me, gathered, groups, left)
     square_list = from_all(squares, "narrow")

time: 75.9 us -> 70.8 us (0.933)
  local copies, waits for them, and re-layouts: 2.88 us -> 0.73 us
  waiting for transfers between devices: 4.04 us -> 2.2 us
  Pallas kernels: 53.3 us -> 52.2 us
    unnamed x29 -> x27, local copies, waits for them, and re-layouts: 2.87 us -> 0.72 us
    ppermute x15, waiting for transfers between devices: 4.04 us -> 2.2 us  [exchanged(): lax.ppermute(value, axis, [(i, i ^ mask) for i in range(lax.axis_size(axi...]
    pallas_call x2, Pallas kernels: 27.4 us -> 26.4 us  [proj(): pl.pallas_call(functools.partial(proj_kernel, slots=slots, first=first, n...]
  transfers between devices with their start and end apart: 15 -> 15, of which waited for: 2 -> 2; matrix products, arithmetic and copies ran while one was open for 0% -> 0% of each run, Pallas kernels for 49% -> 52%
where the time goes in v3:
time: 70.8 us; the launch traced here: 70.6 us
  Pallas kernels  52.2 us (74%)
  starting transfers between devices  13.8 us (19%)
  waiting for transfers between devices  2.2 us (3%)
  between operations  0.98 us (1%)
  local copies, waits for them, and re-layouts  0.73 us (1%)
  other arithmetic  0.71 us (1%)
    pallas_call x2, Pallas kernels, proj(): pl.pallas_call(functools.partial(proj_kernel, slots=slots, first=first, n...  26.4 us
    ppermute x15, starting transfers between devices, exchanged(): lax.ppermute(value, axis, [(i, i ^ mask) for i in range(lax.axis_size(axi...  13.8 us
    pallas_call x2, Pallas kernels, state_write(): pl.pallas_call(functools.partial(state_write_kernel, groups=groups, heads...  11.1 us
    pallas_call x1, Pallas kernels, out_proj(): pl.pallas_call(functools.partial(out_proj_kernel, wide=wide, groups=group...  6.95 us
    pallas_call x1, Pallas kernels, state_read(): pl.pallas_call(functools.partial(state_read_kernel, groups=groups), out_s...  2.83 us
    ppermute x15, waiting for transfers between devices, exchanged(): lax.ppermute(value, axis, [(i, i ^ mask) for i in range(lax.axis_size(axi...  2.2 us
    pallas_call x1, Pallas kernels, kept_channels(): pl.pallas_call(kept_channels_kernel, out_shape=jax.ShapeDtypeStruct(histo...  1.65 us
  transfers between devices with their start and end apart: 15, of which 2 were waited for; matrix products, arithmetic and copies ran while one was open for 0% of the time, Pallas kernels for 52%

profile of v3, /device:TPU:0, one launch (start us, length us, event | category | flops | bytes accessed | tf_op | source)
XLA Modules:
  0.0 70.6 jit_solution(8545933720676035101)
XLA Ops:
  0.6 0.0 copy-start.1
  0.7 0.7 pad_add_fusion.refs_0_.me_ref
  1.4 13.2 %proj_small.1 = (bf16[96,1152]{1,0:T(8,128)(2,1)}, bf16[96,1152]{1,0:T(8,128)(2,1)}, bf16[96,1152]{1,0:T(8,128)(2,1)}, bf16[96,1152]{1,0:T(8,128)(2,1)}) custom-call(s32[2]{0:T(128)} %pad_add_fusion.refs_0_.me_ref, bf16[2048,32,2,128]{3,2,1,0:T(2,128)(2,1)} %bitcast.30, bf16[20,2,2048]{2,1,0:T(2,128)(2,1)} %refs_2_.3, bf16[2048,1024]{1,0:T(8,128)(2,1)} %refs_3_.1, ...), custom_call_target="tpu_custom_call" | custom-call | flops 1019215872 | bytes 21233664 | tf_op jit(solution)/shard_map/proj_small/pallas_call | solution.py:258
  14.5 0.5 collective-permute-start
  15.0 2.6 %collective-permute-start.1 = (bf16[96,1152]{1,0:T(8,128)(2,1)}, bf16[96,1152]{1,0:T(8,128)(2,1)S(1)}, u32[]{:S(2)}, u32[]{:S(2)}) collective-permute-start(bf16[96,1152]{1,0:T(8,128)(2,1)} %get-tuple-element.32), channel_id=1, source_target_pairs={{0,2},{1,3},{2,0},{3,1},{4,6},{5,7},{6,4},{7,5},{8,10},{9,11},{10,... | collective-permute-start | bytes 663560 | tf_op jit(solution)/shard_map/ppermute | solution.py:33
  17.6 0.1 collective-permute-start.2
  17.7 0.0 copy-start.10
  17.8 13.3 %proj.1 = (f32[20,1024,256]{2,1,0:T(8,128)S(1)}, bf16[80,1024]{1,0:T(8,128)(2,1)S(1)}, bf16[96,512]{1,0:T(8,128)(2,1)S(1)}, bf16[96,512]{1,0:T(8,128)(2,1)S(1)},...) custom-call(s32[2]{0:T(128)S(1)} %copy-done.5, bf16[2048,32,2,128]{3,2,1,0:T(2,128)(2,1)} %bitcast.31, ...), custom_call_target="tpu_custom_call" | custom-call | flops 1811939328 | bytes 37748736 | tf_op jit(solution)/shard_map/proj/pallas_call | solution.py:258
  31.1 0.2 collective-permute-start.3
  31.3 1.9 %collective-permute-start.4 = (bf16[96,512]{1,0:T(8,128)(2,1)S(1)}, bf16[96,512]{1,0:T(8,128)(2,1)S(1)}, u32[]{:S(2)}, u32[]{:S(2)}) collective-permute-start(bf16[96,512]{1,0:T(8,128)(2,1)S(1)} %get-tuple-element.37), channel_id=1, source_target_pairs={{0,2},{1,3},{2,0},{3,1},{4,6},{5,7},{6,4},{7,5},{8,10},{9,11},{10,... | collective-permute-start | bytes 294920 | tf_op jit(solution)/shard_map/ppermute | solution.py:33
  33.2 0.1 collective-permute-start.5
  33.4 0.8 %bc_conv.1 = (f32[48,1024]{1,0:T(8,128)S(1)}, bf16[3,20,1024]{2,1,0:T(8,128)(2,1)}, f32[48,128]{1,0:T(8,128)S(1)}, bf16[96,512]{1,0:T(8,128)(2,1)S(1)}) custom-call(bf16[96,1152]{1,0:T(8,128)(2,1)S(1)} %copy-done.2, bf16[96,1152]{1,0:T(8,128)(2,1)S(1)} %collective-permute-done.refs_1_, bf16[96,1152]{1,0:T(8,128)(2,1)S(1)} %collective-permute-done.1.refs_2_, ...), custom_call_target="tpu_custom_call" | custom-call | flops 2949120 | bytes 786432 | tf_op jit(solution)/shard_map/bc_conv/pallas_call | solution.py:313
  34.2 2.8 %state_read.1.refs_6_ = f32[48,1024]{1,0:T(8,128)S(1)} custom-call(f32[48,1024]{1,0:T(8,128)S(1)} %get-tuple-element.40.bc_ref.refs_7_.refs_2_, f32[20,1024,256]{2,1,0:T(8,128)S(1)} %get-tuple-element.41.state_ref.refs_3_), custom_call_target="tpu_custom_call" | custom-call | flops 20971520 | bytes 20971520 | tf_op jit(solution)/shard_map/state_read/pallas_call | solution.py:346
  37.1 0.0 collective-permute-done.4.refs_3_
  37.1 1.3 %collective-permute-done.5.refs_4_ = bf16[96,512]{1,0:T(8,128)(2,1)S(1)} collective-permute-done((bf16[96,512]{1,0:T(8,128)(2,1)S(1)}, bf16[96,512]{1,0:T(8,128)(2,1)S(1)}, u32[]{:S(2)}, u32[]{:S(2)}) %collective-permute-start.5) | collective-permute-done | bytes 98336 | tf_op jit(solution)/shard_map/ppermute | solution.py:33
  38.4 0.7 readout.1
  39.1 1.6 %collective-permute-start.6 = (bf16[48,1152]{1,0:T(8,128)(2,1)S(1)}, bf16[48,1152]{1,0:T(8,128)(2,1)S(1)}, u32[]{:S(2)}, u32[]{:S(2)}) collective-permute-start(bf16[48,1152]{1,0:T(8,128)(2,1)S(1)} %get-tuple-element.43.refs_0_), channel_id=1, source_target_pairs={{0,4},{4,0},{8,12},{12,8},{1,5},{5,1},{9,13},{13,9},{2,6},{6,2},{1... | collective-permute-start | bytes 331784 | tf_op jit(solution)/shard_map/ppermute | solution.py:33
  40.7 2.6 %collective-permute-start.7 = (bf16[48,1152]{1,0:T(8,128)(2,1)S(1)}, bf16[48,1152]{1,0:T(8,128)(2,1)S(1)}, u32[]{:S(2)}, u32[]{:S(2)}) collective-permute-start(bf16[48,1152]{1,0:T(8,128)(2,1)S(1)} %get-tuple-element.43.refs_0_), channel_id=1, source_target_pairs={{0,8},{4,12},{8,0},{12,4},{1,9},{5,13},{9,1},{13,5},{2,10},{6,14},... | collective-permute-start | bytes 331784 | tf_op jit(solution)/shard_map/ppermute | solution.py:33
  43.3 0.3 collective-permute-start.8
  43.6 7.9 %state_write.2 = (f32[20,1024,256]{2,1,0:T(8,128)}, bf16[1024,256]{1,0:T(8,128)(2,1)S(1)}, f32[1280,128]{1,0:T(8,128)S(1)}) custom-call(f32[48,1024]{1,0:T(8,128)S(1)} %get-tuple-element.44.refs_0_, f32[24,64]{1,0:T(8,128)S(1)} %get-tuple-element.45.refs_1_, f32[48,1024]{1,0:T(8,128)S(1)} %get-tuple-element.40.bc_ref.refs_7_.refs_2_, ...), custom_call_target="tpu_custom_call" | custom-call | flops 16777216 | bytes 33554432 | tf_op jit(solution)/shard_map/state_write/pallas_call | solution.py:518
  51.5 0.8 %collective-permute-done.7.refs_2_ = bf16[48,1152]{1,0:T(8,128)(2,1)S(1)} collective-permute-done((bf16[48,1152]{1,0:T(8,128)(2,1)S(1)}, bf16[48,1152]{1,0:T(8,128)(2,1)S(1)}, u32[]{:S(2)}, u32[]{:S(2)}) %collective-permute-start.7) | collective-permute-done | bytes 110624 | tf_op jit(solution)/shard_map/ppermute | solution.py:33
  52.3 0.7 %all_squares.1.refs_5_.refs_0_ = f32[48,128]{1,0:T(8,128)S(1)} custom-call(s32[2]{0:T(128)S(1)} %copy-done.5, bf16[48,1152]{1,0:T(8,128)(2,1)S(1)} %get-tuple-element.43.refs_0_, bf16[48,1152]{1,0:T(8,128)(2,1)S(1)} %collective-permute-done.6.refs_1_, bf16[48,1152]{1,0:T(8,128)(2,1)S(1)} %collective-permute-done.7.refs_2_, ...), custom_call_target="tpu_custom_call" | custom-call | flops 65536 | bytes 262144 | tf_op jit(solution)/shard_map/all_squares/pallas_call | solution.py:549
  53.0 0.1 collective-permute-start.9
  53.1 1.1 %collective-permute-start.10 = (f32[48,128]{1,0:T(8,128)S(1)}, f32[48,128]{1,0:T(8,128)S(1)}, u32[]{:S(2)}, u32[]{:S(2)}) collective-permute-start(f32[48,128]{1,0:T(8,128)S(1)} %all_squares.1.refs_5_.refs_0_), channel_id=1, source_target_pairs={{0,2},{1,3},{2,0},{3,1},{4,6},{5,7},{6,4},{7,5},{8,10},{9,11},{10,... | collective-permute-start | bytes 73736 | tf_op jit(solution)/shard_map/ppermute | solution.py:33
  54.2 0.8 %collective-permute-start.11 = (f32[48,128]{1,0:T(8,128)S(1)}, f32[48,128]{1,0:T(8,128)S(1)}, u32[]{:S(2)}, u32[]{:S(2)}) collective-permute-start(f32[48,128]{1,0:T(8,128)S(1)} %all_squares.1.refs_5_.refs_0_), channel_id=1, source_target_pairs={{0,3},{1,2},{2,1},{3,0},{4,7},{5,6},{6,5},{7,4},{8,11},{9,10},{10,... | collective-permute-start | bytes 73736 | tf_op jit(solution)/shard_map/ppermute | solution.py:33
  55.0 6.9 %out_proj.1.made_ref = f32[8,48,2048]{2,1,0:T(8,128)S(1)} custom-call(s32[2]{0:T(128)S(1)} %copy-done.5, bf16[48,1152]{1,0:T(8,128)(2,1)S(1)} %get-tuple-element.43.refs_0_, bf16[48,1152]{1,0:T(8,128)(2,1)S(1)} %collective-permute-done.6.refs_1_, bf16[48,1152]{1,0:T(8,128)(2,1)S(1)} %collective-permute-done.7.refs_2_, ...), custom_call_target="tpu_custom_call" | custom-call | flops 805306368 | bytes 16777216 | tf_op jit(solution)/shard_map/out_proj/pallas_call | solution.py:586
  62.0 1.0 %out_scale.1 = (bf16[48,512]{1,0:T(8,128)(2,1)S(1)}, bf16[48,512]{1,0:T(8,128)(2,1)S(1)}, bf16[48,512]{1,0:T(8,128)(2,1)S(1)}, bf16[48,512]{1,0:T(8,128)(2,1)S(1)}) custom-call(s32[2]{0:T(128)S(1)} %copy-done.5, f32[8,48,2048]{2,1,0:T(8,128)S(1)} %out_proj.1.made_ref, f32[48,128]{1,0:T(8,128)S(1)} %all_squares.1.refs_5_.refs_0_, ...), custom_call_target="tpu_custom_call" | custom-call | flops 3145728 | bytes 3145728 | tf_op jit(solution)/shard_map/out_scale/pallas_call | solution.py:622
  62.9 1.0 %collective-permute-start.14 = (bf16[48,512]{1,0:T(8,128)(2,1)S(1)}, bf16[48,512]{1,0:T(8,128)(2,1)S(1)}, u32[]{:S(2)}, u32[]{:S(2)}) collective-permute-start(bf16[48,512]{1,0:T(8,128)(2,1)S(1)} %get-tuple-element.50), channel_id=1, source_target_pairs={{0,3},{1,2},{2,1},{3,0},{4,7},{5,6},{6,5},{7,4},{8,11},{9,10},{10,... | collective-permute-start | bytes 147464 | tf_op jit(solution)/shard_map/ppermute | solution.py:33
  64.0 1.0 %collective-permute-start.13 = (bf16[48,512]{1,0:T(8,128)(2,1)S(1)}, bf16[48,512]{1,0:T(8,128)(2,1)S(1)}, u32[]{:S(2)}, u32[]{:S(2)}) collective-permute-start(bf16[48,512]{1,0:T(8,128)(2,1)S(1)} %get-tuple-element.49), channel_id=1, source_target_pairs={{0,2},{1,3},{2,0},{3,1},{4,6},{5,7},{6,4},{7,5},{8,10},{9,11},{10,... | collective-permute-start | bytes 147464 | tf_op jit(solution)/shard_map/ppermute | solution.py:33
  65.0 1.6 %kept_channels.1 = bf16[20,3,16,64]{3,2,1,0:T(8,128)(2,1)} custom-call(bf16[20,3,16,64]{3,2,1,0:T(8,128)(2,1)S(1)} %bitcast.25, bf16[48,1024]{1,0:T(8,128)(2,1)S(1)} %get-tuple-element.54.fresh_ref), custom_call_target="tpu_custom_call" | custom-call | flops 4915200 | bytes 196608 | tf_op jit(solution)/shard_map/kept_channels/pallas_call | solution.py:97
  66.6 3.2 %state_write.3 = (f32[20,1024,256]{2,1,0:T(8,128)}, f32[8,128]{1,0:T(8,128)}) custom-call(bf16[1024,256]{1,0:T(8,128)(2,1)S(1)} %get-tuple-element.46.refs_4_.refs_0_, f32[1280,128]{1,0:T(8,128)S(1)} %get-tuple-element.51.refs_1_, f32[48,1024]{1,0:T(8,128)S(1)} %get-tuple-element.40.bc_ref.refs_7_.refs_2_, ...), custom_call_target="tpu_custom_call", output_to_operand_aliasing={{0}: (4, {})} | custom-call | flops 4194304 | bytes 8388608 | tf_op jit(solution)/shard_map/state_write/pallas_call | solution.py:518
  69.9 0.6 copy.24
  (40 shorter events, 0.1 us)
Async XLA Ops:
  0.6 17.0 %copy-start.1 = (bf16[20,2,2048]{2,1,0:T(2,128)(2,1)S(1)}, bf16[20,2,2048]{2,1,0:T(2,128)(2,1)}, u32[]{:S(2)}) copy-start(bf16[20,2,2048]{2,1,0:T(2,128)(2,1)} %refs_2_.3) | copy-start | bytes 491524
  0.6 17.0 %copy-start = (bf16[20,3,64,16]{2,3,1,0:T(8,128)(2,1)S(1)}, bf16[20,3,64,16]{2,3,1,0:T(8,128)(2,1)}, u32[]{:S(2)}) copy-start(bf16[20,3,64,16]{2,3,1,0:T(8,128)(2,1)} %param.24) | copy-start | bytes 368644
  0.7 17.0 %copy-start.4 = (bf16[4,64,16]{1,2,0:T(8,128)(2,1)S(1)}, bf16[4,64,16]{1,2,0:T(8,128)(2,1)}, u32[]{:S(2)}) copy-start(bf16[4,64,16]{1,2,0:T(8,128)(2,1)} %param.20) | copy-start | bytes 24580
  0.7 17.0 %copy-start.7 = (bf16[64,16]{0,1:T(8,128)(2,1)S(1)}, bf16[64,16]{0,1:T(8,128)(2,1)}, u32[]{:S(2)}) copy-start(bf16[64,16]{0,1:T(8,128)(2,1)} %param.21) | copy-start | bytes 6148
  0.7 17.0 %copy-start.8 = (bf16[64,16]{0,1:T(8,128)(2,1)S(1)}, bf16[64,16]{0,1:T(8,128)(2,1)}, u32[]{:S(2)}) copy-start(bf16[64,16]{0,1:T(8,128)(2,1)} %param.29) | copy-start | bytes 6148
  1.4 16.4 %copy-start.5 = (s32[2]{0:T(128)S(1)}, s32[2]{0:T(128)}, u32[]{:S(2)}) copy-start(s32[2]{0:T(128)} %pad_add_fusion.refs_0_.me_ref) | copy-start | bytes 28
  14.5 18.7 %collective-permute-start = (bf16[96,1152]{1,0:T(8,128)(2,1)}, bf16[96,1152]{1,0:T(8,128)(2,1)S(1)}, u32[]{:S(2)}, u32[]{:S(2)}) collective-permute-start(bf16[96,1152]{1,0:T(8,128)(2,1)} %get-tuple-element.31), channel_id=1, source_target_pairs={{0,1},{1,0},{2,3},{3,2},{4,5},{5,4},{6,7},{7,6},{8,9},{9,8},{10,11... | collective-permute-start | bytes 663560 | tf_op jit(solution)/shard_map/ppermute | solution.py:33
  15.0 18.3 %collective-permute-start.1 = (bf16[96,1152]{1,0:T(8,128)(2,1)}, bf16[96,1152]{1,0:T(8,128)(2,1)S(1)}, u32[]{:S(2)}, u32[]{:S(2)}) collective-permute-start(bf16[96,1152]{1,0:T(8,128)(2,1)} %get-tuple-element.32), channel_id=1, source_target_pairs={{0,2},{1,3},{2,0},{3,1},{4,6},{5,7},{6,4},{7,5},{8,10},{9,11},{10,... | collective-permute-start | bytes 663560 | tf_op jit(solution)/shard_map/ppermute | solution.py:33
  17.6 15.8 %collective-permute-start.2 = (bf16[96,1152]{1,0:T(8,128)(2,1)}, bf16[96,1152]{1,0:T(8,128)(2,1)S(1)}, u32[]{:S(2)}, u32[]{:S(2)}) collective-permute-start(bf16[96,1152]{1,0:T(8,128)(2,1)} %get-tuple-element.33), channel_id=1, source_target_pairs={{0,3},{1,2},{2,1},{3,0},{4,7},{5,6},{6,5},{7,4},{8,11},{9,10},{10,... | collective-permute-start | bytes 663560 | tf_op jit(solution)/shard_map/ppermute | solution.py:33
  17.7 15.5 %copy-start.9 = (bf16[1024]{0:T(1024)(128)(2,1)S(1)}, bf16[1024]{0:T(1024)(128)(2,1)}, u32[]{:S(2)}) copy-start(bf16[1024]{0:T(1024)(128)(2,1)} %param.23) | copy-start | bytes 6148
  17.7 15.6 %copy-start.10 = (f32[64]{0:T(128)S(1)}, f32[64]{0:T(128)}, u32[]{:S(2)}) copy-start(f32[64]{0:T(128)} %param.28) | copy-start | bytes 772
  17.7 15.6 %copy-start.11 = (f32[64]{0:T(128)S(1)}, f32[64]{0:T(128)}, u32[]{:S(2)}) copy-start(f32[64]{0:T(128)} %param.27) | copy-start | bytes 772
  17.7 15.6 %copy-start.12 = (f32[64]{0:T(128)S(1)}, f32[64]{0:T(128)}, u32[]{:S(2)}) copy-start(f32[64]{0:T(128)} %param.26) | copy-start | bytes 772
  17.8 15.6 %copy-start.2 = (bf16[96,1152]{1,0:T(8,128)(2,1)S(1)}, bf16[96,1152]{1,0:T(8,128)(2,1)}, u32[]{:S(2)}) copy-start(bf16[96,1152]{1,0:T(8,128)(2,1)} %get-tuple-element.30.refs_0_) | copy-start | bytes 663556
  17.8 15.6 %copy-start.3 = (bf16[20,3,1024]{2,0,1:T(8,128)(2,1)S(1)}, bf16[20,3,1024]{2,0,1:T(8,128)(2,1)}, u32[]{:S(2)}) copy-start(bf16[20,3,1024]{2,0,1:T(8,128)(2,1)} %param.25) | copy-start | bytes 368644
  17.8 15.6 %copy-start.6 = (bf16[4,1024]{1,0:T(4,128)(2,1)S(1)}, bf16[4,1024]{1,0:T(4,128)(2,1)}, u32[]{:S(2)}) copy-start(bf16[4,1024]{1,0:T(4,128)(2,1)} %refs_5_.1) | copy-start | bytes 24580
  31.1 6.0 %collective-permute-start.3 = (bf16[96,512]{1,0:T(8,128)(2,1)S(1)}, bf16[96,512]{1,0:T(8,128)(2,1)S(1)}, u32[]{:S(2)}, u32[]{:S(2)}) collective-permute-start(bf16[96,512]{1,0:T(8,128)(2,1)S(1)} %get-tuple-element.36), channel_id=1, source_target_pairs={{0,1},{1,0},{2,3},{3,2},{4,5},{5,4},{6,7},{7,6},{8,9},{9,8},{10,11... | collective-permute-start | bytes 294920 | tf_op jit(solution)/shard_map/ppermute | solution.py:33
  31.3 5.8 %collective-permute-start.4 = (bf16[96,512]{1,0:T(8,128)(2,1)S(1)}, bf16[96,512]{1,0:T(8,128)(2,1)S(1)}, u32[]{:S(2)}, u32[]{:S(2)}) collective-permute-start(bf16[96,512]{1,0:T(8,128)(2,1)S(1)} %get-tuple-element.37), channel_id=1, source_target_pairs={{0,2},{1,3},{2,0},{3,1},{4,6},{5,7},{6,4},{7,5},{8,10},{9,11},{10,... | collective-permute-start | bytes 294920 | tf_op jit(solution)/shard_map/ppermute | solution.py:33
  33.2 5.2 %collective-permute-start.5 = (bf16[96,512]{1,0:T(8,128)(2,1)S(1)}, bf16[96,512]{1,0:T(8,128)(2,1)S(1)}, u32[]{:S(2)}, u32[]{:S(2)}) collective-permute-start(bf16[96,512]{1,0:T(8,128)(2,1)S(1)} %get-tuple-element.38), channel_id=1, source_target_pairs={{0,3},{1,2},{2,1},{3,0},{4,7},{5,6},{6,5},{7,4},{8,11},{9,10},{10,... | collective-permute-start | bytes 294920 | tf_op jit(solution)/shard_map/ppermute | solution.py:33
  39.1 12.4 %collective-permute-start.6 = (bf16[48,1152]{1,0:T(8,128)(2,1)S(1)}, bf16[48,1152]{1,0:T(8,128)(2,1)S(1)}, u32[]{:S(2)}, u32[]{:S(2)}) collective-permute-start(bf16[48,1152]{1,0:T(8,128)(2,1)S(1)} %get-tuple-element.43.refs_0_), channel_id=1, source_target_pairs={{0,4},{4,0},{8,12},{12,8},{1,5},{5,1},{9,13},{13,9},{2,6},{6,2},{1... | collective-permute-start | bytes 331784 | tf_op jit(solution)/shard_map/ppermute | solution.py:33
  40.7 11.6 %collective-permute-start.7 = (bf16[48,1152]{1,0:T(8,128)(2,1)S(1)}, bf16[48,1152]{1,0:T(8,128)(2,1)S(1)}, u32[]{:S(2)}, u32[]{:S(2)}) collective-permute-start(bf16[48,1152]{1,0:T(8,128)(2,1)S(1)} %get-tuple-element.43.refs_0_), channel_id=1, source_target_pairs={{0,8},{4,12},{8,0},{12,4},{1,9},{5,13},{9,1},{13,5},{2,10},{6,14},... | collective-permute-start | bytes 331784 | tf_op jit(solution)/shard_map/ppermute | solution.py:33
  43.3 9.0 %collective-permute-start.8 = (bf16[48,1152]{1,0:T(8,128)(2,1)S(1)}, bf16[48,1152]{1,0:T(8,128)(2,1)S(1)}, u32[]{:S(2)}, u32[]{:S(2)}) collective-permute-start(bf16[48,1152]{1,0:T(8,128)(2,1)S(1)} %get-tuple-element.43.refs_0_), channel_id=1, source_target_pairs={{0,12},{4,8},{8,4},{12,0},{1,13},{5,9},{9,5},{13,1},{2,14},{6,10},... | collective-permute-start | bytes 331784 | tf_op jit(solution)/shard_map/ppermute | solution.py:33
  53.0 8.9 %collective-permute-start.9 = (f32[48,128]{1,0:T(8,128)S(1)}, f32[48,128]{1,0:T(8,128)S(1)}, u32[]{:S(2)}, u32[]{:S(2)}) collective-permute-start(f32[48,128]{1,0:T(8,128)S(1)} %all_squares.1.refs_5_.refs_0_), channel_id=1, source_target_pairs={{0,1},{1,0},{2,3},{3,2},{4,5},{5,4},{6,7},{7,6},{8,9},{9,8},{10,11... | collective-permute-start | bytes 73736 | tf_op jit(solution)/shard_map/ppermute | solution.py:33
  53.1 8.8 %collective-permute-start.10 = (f32[48,128]{1,0:T(8,128)S(1)}, f32[48,128]{1,0:T(8,128)S(1)}, u32[]{:S(2)}, u32[]{:S(2)}) collective-permute-start(f32[48,128]{1,0:T(8,128)S(1)} %all_squares.1.refs_5_.refs_0_), channel_id=1, source_target_pairs={{0,2},{1,3},{2,0},{3,1},{4,6},{5,7},{6,4},{7,5},{8,10},{9,11},{10,... | collective-permute-start | bytes 73736 | tf_op jit(solution)/shard_map/ppermute | solution.py:33
  54.2 7.8 %collective-permute-start.11 = (f32[48,128]{1,0:T(8,128)S(1)}, f32[48,128]{1,0:T(8,128)S(1)}, u32[]{:S(2)}, u32[]{:S(2)}) collective-permute-start(f32[48,128]{1,0:T(8,128)S(1)} %all_squares.1.refs_5_.refs_0_), channel_id=1, source_target_pairs={{0,3},{1,2},{2,1},{3,0},{4,7},{5,6},{6,5},{7,4},{8,11},{9,10},{10,... | collective-permute-start | bytes 73736 | tf_op jit(solution)/shard_map/ppermute | solution.py:33
  62.9 6.9 %collective-permute-start.14 = (bf16[48,512]{1,0:T(8,128)(2,1)S(1)}, bf16[48,512]{1,0:T(8,128)(2,1)S(1)}, u32[]{:S(2)}, u32[]{:S(2)}) collective-permute-start(bf16[48,512]{1,0:T(8,128)(2,1)S(1)} %get-tuple-element.50), channel_id=1, source_target_pairs={{0,3},{1,2},{2,1},{3,0},{4,7},{5,6},{6,5},{7,4},{8,11},{9,10},{10,... | collective-permute-start | bytes 147464 | tf_op jit(solution)/shard_map/ppermute | solution.py:33
  64.0 5.9 %collective-permute-start.13 = (bf16[48,512]{1,0:T(8,128)(2,1)S(1)}, bf16[48,512]{1,0:T(8,128)(2,1)S(1)}, u32[]{:S(2)}, u32[]{:S(2)}) collective-permute-start(bf16[48,512]{1,0:T(8,128)(2,1)S(1)} %get-tuple-element.49), channel_id=1, source_target_pairs={{0,2},{1,3},{2,0},{3,1},{4,6},{5,7},{6,4},{7,5},{8,10},{9,11},{10,... | collective-permute-start | bytes 147464 | tf_op jit(solution)/shard_map/ppermute | solution.py:33
  65.0 4.9 %collective-permute-start.12 = (bf16[48,512]{1,0:T(8,128)(2,1)S(1)}, bf16[48,512]{1,0:T(8,128)(2,1)S(1)}, u32[]{:S(2)}, u32[]{:S(2)}) collective-permute-start(bf16[48,512]{1,0:T(8,128)(2,1)S(1)} %get-tuple-element.48), channel_id=1, source_target_pairs={{0,1},{1,0},{2,3},{3,2},{4,5},{5,4},{6,7},{7,6},{8,9},{9,8},{10,11... | collective-permute-start | bytes 147464 | tf_op jit(solution)/shard_map/ppermute | solution.py:33
